TPU v7x, 512 devices: a whole 4x8x8 slice. The times are simulated.
512 devices in a mesh: blk: 32 (over y, x_lo, core), rep: 16 (over z, x_hi).
Axes of the slice: x: 4 (x_hi: 2, x_lo: 2; x = x_hi * 2 + x_lo), y: 8, z: 8, core: 2. Of those that a mesh axis runs over, the one named last changes fastest.
Arguments:
- visit_embeds: bfloat16 [16, 4096, 1024], P('rep', 'blk'), may hold values from -6 to 6
- result_embeds: bfloat16 [16, 4096, 1024], P('rep', 'blk'), may hold values from -6 to 6
- matched_result_index: int32 [16, 4096], P('rep'), may hold values from 0 to 4095, each once within a row
- logit_stretch: float32 [], replicated, may hold values from 1 to 3
- logit_offset: float32 [], replicated, may hold values from -4 to -1
Outputs:
- d_sessions: float32 [16, 4096, 1024], P('rep', 'blk')
- d_outcomes: float32 [16, 4096, 1024], P('rep', 'blk')
- loss: float32 [], replicated
- d_temperature: float32 [], replicated
- d_bias: float32 [], replicated
Inputs may be any that keep to these rules, and one draw needn't show every extreme that they name: `matched_result_index`: each row names every outcome of its batch exactly once.
All inputs are finite; a program needn't handle non-finite values.
Results may differ from a plain program's by a relative error of at most 0.002.
Values may be sent and summed in bfloat16 or wider, within the bound.
No kernel may reach another device: no remote copies, remote signals or barrier semaphores. Data moves between devices by JAX's collectives and lax.ppermute only.
A program may use at most 64 MiB of HBM per device.

v0:
```python
import math

import jax
import jax.numpy as jnp
from jax import lax
from jax.sharding import PartitionSpec as P


def couple_contributions(
    leading_argument,
    trailing_argument,
    indicator_grid,
    target_indicator,
    logit_stretch,
    logit_offset,
):
    stretch_multiplier = 1.0 / math.sqrt(leading_argument.shape[1])
    following_entry = (
        lax.dot_general(
            leading_argument,
            trailing_argument,
            (((1,), (1,)), ((), ())),
            preferred_element_type=jnp.float32,
        )
        * stretch_multiplier
    )
    initial_entry = logit_stretch * following_entry + logit_offset
    z_val = jnp.where(indicator_grid[:, None] == target_indicator[None, :], 1.0, -1.0).astype(
        jnp.float32
    )
    derivative_entry = -z_val * jax.nn.sigmoid(-z_val * initial_entry)
    multiplier = (derivative_entry * (logit_stretch * stretch_multiplier)).astype(jnp.bfloat16)
    return (following_entry, initial_entry, z_val, derivative_entry, multiplier)


def local(visit_embeds, result_embeds, matched_result_index, logit_stretch, logit_offset):
    resident_visits = visit_embeds[0]
    resident_results = result_embeds[0]
    entire_indicator = matched_result_index[0]
    rows = resident_visits.shape[0]
    first_row = lax.axis_index("blk") * rows
    resident_indicator = lax.dynamic_slice_in_dim(entire_indicator, first_row, rows)
    resident_targets = first_row + jnp.arange(rows, dtype=jnp.int32)
    submatrix_piece = lax.all_gather(result_embeds, "blk", axis=1, tiled=True)[0]
    number_entries = submatrix_piece.shape[0]
    target_indicator = jnp.arange(number_entries, dtype=jnp.int32)
    following_entry, initial_entry, z_val, derivative_entry, multiplier = couple_contributions(
        resident_visits,
        submatrix_piece,
        resident_indicator,
        target_indicator,
        logit_stretch,
        logit_offset,
    )
    visit_derivative = jnp.dot(multiplier, submatrix_piece, preferred_element_type=jnp.float32)
    objective_accumulated = jnp.sum(jax.nn.softplus(-z_val * initial_entry))
    visit_derivative, objective_accumulated, stretch_accumulated, offset_accumulated = (
        visit_derivative,
        objective_accumulated,
        jnp.sum(derivative_entry * following_entry),
        jnp.sum(derivative_entry),
    )
    submatrix_piece = lax.all_gather(visit_embeds, "blk", axis=1, tiled=True)[0]
    following_entry, initial_entry, z_val, derivative_entry, multiplier = couple_contributions(
        submatrix_piece,
        resident_results,
        entire_indicator,
        resident_targets,
        logit_stretch,
        logit_offset,
    )
    result_derivative = lax.dot_general(
        multiplier, submatrix_piece, (((0,), (0,)), ((), ())), preferred_element_type=jnp.float32
    )
    objective_accumulated, stretch_accumulated, offset_accumulated = lax.psum(
        (objective_accumulated, stretch_accumulated, offset_accumulated), ("blk", "rep")
    )
    batch = entire_indicator.shape[0]
    number_entries = 1.0 * lax.axis_size("rep") * batch * batch
    return (
        visit_derivative[None],
        result_derivative[None],
        objective_accumulated / number_entries,
        stretch_accumulated / number_entries,
        offset_accumulated / number_entries,
    )


def solution(mesh):
    in_specs = (P("rep", "blk", None), P("rep", "blk", None), P("rep", None), P(), P())
    out_specs = (P("rep", "blk", None), P("rep", "blk", None), P(), P(), P())
    return jax.shard_map(local, mesh=mesh, in_specs=in_specs, out_specs=out_specs, check_vma=False)
```

profile of v0, /device:TPU:1, one launch (start us, length us, event | category | flops | bytes accessed | tf_op | source)
XLA Modules:
  0.0 227.6 jit_solution(2788016338427516617)
XLA Ops:
  7.2 0.0 all-gather.3.cloned.1.call-start
  7.2 0.7 all-gather.3.cloned.1.call-update
  7.9 0.0 all-gather.5.cloned.1.call-start
  7.9 0.7 all-gather.5.cloned.1.call-update
  10.0 0.7 dynamic-slice_bitcast_fusion
  10.6 80.5 %all-gather.3.cloned.1.call-done = bf16[1,4096,1024]{2,1,0:T(8,128)(2,1)} async-done(((bf16[1,128,1024]{2,1,0:T(8,128)(2,1)}), bf16[1,4096,1024]{2,1,0:T(8,128)(2,1)}) %all-gather.3.cloned.1.call-update) | async-done | bytes 8388624 | tf_op jit(solution)/shard_map/all_gather | solution.py:44
  91.1 7.8 %fusion.64 = (f32[]{:T(128)}, f32[]{:T(128)}, f32[]{:T(128)}, f32[128,4096]{1,0:T(8,128)S(1)}) fusion(f32[]{:T(128)S(6)} %copy.11, f32[]{:T(128)S(6)} %mul.52, s32[128]{0:T(128)S(1)} %dynamic-slice_bitcast_fusion, bf16[1,4096,1024]{2,1,0:T(8,128)(2,1)} %all-gather.3.cloned.1.call-done, bf16[1,128,1024]{2,1,0:T(8,128)(2,1)} %param.5), kind=kOutput, calls=%fused_computation.44 | convolution fusion | flops 1084751872 | bytes 10748436 | tf_op jit(solution)/shard_map/dot_general | solution.py:19
  98.9 98.3 %all-reduce = (f32[]{:T(128)}, f32[]{:T(128)}, f32[]{:T(128)}) all-reduce(f32[]{:T(128)} %get-tuple-element.7, f32[]{:T(128)} %get-tuple-element.6, f32[]{:T(128)} %get-tuple-element.5), channel_id=1, replica_groups=mesh['blk'=32,'rep'=16] {'blk','rep'}, use_global_device_ids=true, to_apply=%region_1.2 | all-reduce | flops 3 | bytes 24 | tf_op jit(solution)/shard_map/psum | solution.py:75
  199.1 0.0 copy-start
  199.1 0.0 copy-start.1
  199.1 6.2 %fusion.49 = f32[1,128,1024]{2,1,0:T(8,128)} fusion(bf16[1,4096,1024]{2,1,0:T(8,128)(2,1)} %all-gather.3.cloned.1.call-done, f32[]{:T(128)S(6)} %mul.52, f32[128,4096]{1,0:T(8,128)S(1)} %get-tuple-element.11, f32[]{:T(128)S(6)} %copy.11, s32[128]{0:T(128)S(1)} %dynamic-slice_bitcast_fusion), kind=kOutput, calls=%fused_computation.30 | convolution fusion | flops 1080033280 | bytes 11010568 | tf_op jit(solution)/shard_map/dot_general | solution.py:55
  205.3 0.0 all-gather.5.cloned.1.call-done
  205.3 0.0 copy-done
  205.3 0.0 copy-done.1
  205.3 12.0 %fusion.44 = f32[1,128,1024]{2,1,0:T(8,128)} fusion(bf16[1,4096,1024]{2,1,0:T(8,128)(2,1)} %all-gather.5.cloned.1.call-done, f32[]{:T(128)S(6)} %copy.11, f32[]{:T(128)S(6)} %mul.52, s32[128]{0:T(128)S(1)} %iota_add_fusion, s32[4096]{0:T(1024)S(1)} %bitcast.56, bf16[1,128,1024]{2,1,0:T(8,128)(2,1)S(1)} %copy-done), kind=kOutput, calls=%fused_computation.29 | convolution fusion | flops 2153775104 | bytes 9191944 | tf_op jit(solution)/shard_map/dot_general | solution.py:72
  (1 shorter events, 0.0 us)
Async XLA Ops:
  7.2 84.0 %all-gather.3.cloned.1.call-start = ((), (), s32[]{:S(2)}) async-start(), calls=%async_computation | async-start | bytes 8650752 | tf_op jit(solution)/shard_map/all_gather | solution.py:44
  7.9 197.4 %all-gather.5.cloned.1.call-start = ((), (), s32[]{:S(2)}) async-start(), calls=%async_computation.1 | async-start | bytes 8650752 | tf_op jit(solution)/shard_map/all_gather | solution.py:63
  199.1 6.2 %copy-start = (bf16[1,128,1024]{2,1,0:T(8,128)(2,1)S(1)}, bf16[1,128,1024]{2,1,0:T(8,128)(2,1)}, u32[]{:S(2)}) copy-start(bf16[1,128,1024]{2,1,0:T(8,128)(2,1)} %param.6) | copy-start | bytes 786436
  199.1 6.2 %copy-start.1 = (s32[1,4096]{1,0:T(1,128)S(1)}, s32[1,4096]{1,0:T(1,128)}, u32[]{:S(2)}) copy-start(s32[1,4096]{1,0:T(1,128)} %param.7) | copy-start | bytes 49156
Sparse Core Ops, SparseCore 0:
  10.1 80.9 all-gather.2
  93.3 74.8 all-gather.4
where the time goes:
time: 228 us
  blocking collectives  98.3 us (43%)
  waiting for transfers between devices  81.9 us (36%)
  matrix products  25.9 us (11%)
  between operations  20.7 us (9%)
    psum x1, blocking collectives, local(): lax.psum((objective_accumulated, stretch_accumulated, offset_accumulated)...  98.3 us
    all_gather x1, waiting for transfers between devices, local(): lax.all_gather(result_embeds, 'blk', axis=1, tiled=True)[0]  80.5 us
    dot_general x1, matrix products, local(): lax.dot_general(multiplier, submatrix_piece, (((0,), (0,)), ((), ())), pr...  12 us
    dot_general x1, matrix products, couple_contributions(): lax.dot_general(leading_argument, trailing_argument, (((1,), (1,)), ((),...  7.75 us
    dot_general x1, matrix products, local(): jnp.dot(multiplier, submatrix_piece, preferred_element_type=jnp.float32)  6.18 us
  transfers between devices with their start and end apart: 2, of which 1 were waited for; matrix products, arithmetic and copies ran while one was open for 6% of the time, Pallas kernels for 0%

commit v1 on v0

v1 whole, which is shorter than its diff:
```python
import functools
import math

import jax
import jax.numpy as jnp
from jax import lax
from jax.experimental import pallas as pl
from jax.experimental.pallas import tpu as pltpu
from jax.sharding import Mesh
from jax.sharding import PartitionSpec as P

NY, NX, NC, NZ, NH = 8, 2, 2, 8, 2
BLK, REP = ("y", "x", "c"), ("z", "h")


def at(y, x, c):
    return (y % NY) * NX * NC + (x % NX) * NC + (c % NC)


def move(dy=0, dx=0, dc=0):
    return [
        (at(y, x, c), at(y + dy, x + dx, c + dc))
        for y in range(NY)
        for x in range(NX)
        for c in range(NC)
    ]


def split(step):
    return [
        (at(y, x, c), at(y + (step if c == 0 else -step), x, c))
        for y in range(NY)
        for x in range(NX)
        for c in range(NC)
    ]


def pair_kernel(unit, first, n, base_ref, to_ref, scal_ref, idx_ref, v_ref, *rest):
    r_refs, rest = rest[:n], rest[n:]
    if not first:
        ds_in, sums_in, _, *rest = rest
    ds_ref, sums_ref, do_ref, held, sems = rest
    stretch = scal_ref[0]
    offset = scal_ref[1]
    scale = stretch * unit
    matched = idx_ref[...]
    m = v_ref.shape[0]
    width = r_refs[0].shape[0]
    v = v_ref[...]
    sums = [jnp.zeros((8, m), jnp.float32) for _ in range(3)]
    copies = []
    for k, r_ref in enumerate(r_refs):
        r = r_ref[...]
        y = (
            lax.dot_general(r, v, (((1,), (1,)), ((), ())), preferred_element_type=jnp.float32)
            * unit
        )
        x = stretch * y + offset
        hit = base_ref[k] + lax.broadcasted_iota(jnp.int32, (width, m), 0) == matched
        t = jnp.where(hit, -x, x)
        e = jnp.exp(-jnp.abs(t))
        inv = 1.0 / (1.0 + e)
        sig = jnp.where(t >= 0, inv, e * inv)
        grad = jnp.where(hit, -sig, sig)
        for i, a in enumerate((jnp.maximum(t, 0.0) + jnp.log1p(e), grad * y, grad)):
            sums[i] += jnp.sum(a.reshape(width // 8, 8, m), axis=0)
        coef = (grad * scale).astype(jnp.bfloat16)
        slot = k % 2
        if k >= 2:
            copies[k - 2].wait()
        held[slot] = jnp.dot(coef, v, preferred_element_type=jnp.float32)
        rows = pl.ds(pl.multiple_of(to_ref[k] * width, width), width)
        copies.append(pltpu.make_async_copy(held.at[slot], do_ref.at[rows], sems.at[slot]))
        copies[k].start()
        part = lax.dot_general(
            coef, r, (((0,), (0,)), ((), ())), preferred_element_type=jnp.float32
        )
        if k:
            ds_ref[...] += part
        elif first:
            ds_ref[...] = part
        else:
            ds_ref[...] = ds_in[...] + part
    for i, a in enumerate(sums):
        s = a[:, :128]
        for j in range(128, m, 128):
            s += a[:, j : j + 128]
        s = jnp.sum(s, axis=0, keepdims=True)
        sums_ref[i : i + 1, :] = s if first else s + sums_in[i : i + 1, :]
    for copy in copies[-2:]:
        copy.wait()


def pairs(base, to, scal, idx, v, rs, carry=()):
    m, d = v.shape
    width = rs[0].shape[0]
    n = len(rs)
    cols = n * width
    vm = pl.BlockSpec(memory_space=pltpu.VMEM)
    sm = pl.BlockSpec(memory_space=pltpu.SMEM)
    hbm = pl.BlockSpec(memory_space=pl.ANY)
    args = [base, to, scal, idx, v, *rs, *carry]
    first = len(args) - 3
    return pl.pallas_call(
        functools.partial(pair_kernel, 1.0 / math.sqrt(d), not carry, n),
        out_shape=[
            jax.ShapeDtypeStruct((m, d), jnp.float32),
            jax.ShapeDtypeStruct((3, 128), jnp.float32),
            jax.ShapeDtypeStruct((NY * width, d), jnp.float32),
        ],
        in_specs=[sm, sm, sm] + [vm] * (2 + n) + ([vm, vm, hbm] if carry else []),
        out_specs=[vm, vm, hbm],
        scratch_shapes=[
            pltpu.VMEM((2, width, d), jnp.float32),
            pltpu.SemaphoreType.DMA((2,)),
        ],
        input_output_aliases={first + i: i for i in range(3)} if carry else {},
        compiler_params=pltpu.CompilerParams(vmem_limit_bytes=48 * 1024 * 1024),
        cost_estimate=pl.CostEstimate(
            flops=6 * m * cols * d,
            bytes_accessed=2 * (m + cols) * d + 4 * (2 * m + cols) * d,
            transcendentals=3 * m * cols,
        ),
    )(*args)


def local(visit_embeds, result_embeds, matched_result_index, logit_stretch, logit_offset):
    v0 = visit_embeds[0]
    r0 = result_embeds[0]
    rows = v0.shape[0]
    index = matched_result_index[0]
    batch = index.shape[0]
    me = lax.axis_index(BLK)
    y, x, c = me // (NX * NC), (me // NC) % NX, me % NC
    tie = lambda *xs: lax.optimization_barrier(xs)
    send = lambda a, p: lax.ppermute(a, BLK, p)
    right, left = move(dy=1), move(dy=-1)

    v = jnp.concatenate([v0, send(v0, move(dc=1))], axis=0)
    l1, u1 = send(r0, right), send(r0, left)
    v = jnp.concatenate([v, send(v, move(dx=1))], axis=0)
    l2, u2 = send(l1, right), send(u1, left)

    scal = jnp.stack([logit_stretch, logit_offset])
    idx = jnp.concatenate(
        [
            lax.dynamic_slice_in_dim(index, at(y, x + a, c + o) * rows, rows)
            for a in (0, 1)
            for o in (0, 1)
        ]
    )[None]

    def work(steps, rs, carry=()):
        to = jnp.stack([(y + k) % NY for k in steps]).astype(jnp.int32)
        base = (to * (NX * NC) + x * NC + c) * rows
        return pairs(base.astype(jnp.int32), to, scal, idx, v, rs, carry)

    carry = work((0, -1, 1), (r0, l1, u1))
    l2, u2, *carry = tie(l2, u2, *carry)
    l3, u3 = send(l2, right), send(u2, left)
    carry = work((-2, 2), (l2, u2), carry)
    l3, u3, *carry = tie(l3, u3, *carry)
    r4 = send(jnp.where(c == 0, l3, u3), split(1))
    carry = work((-3, 3), (l3, u3), carry)
    ds, sums, do = work((4,), (r4,), carry)

    do = lax.psum_scatter(do, "y", scatter_dimension=0, tiled=True)
    dx = send(ds[2 * rows :], move(dx=1))
    sums = lax.psum(sums, "c")
    sums = lax.psum(sums, "z")
    sums, dx = tie(sums, dx)
    ds = ds[: 2 * rows] + dx
    dc = send(ds[rows:], move(dc=1))
    sums = lax.psum(sums, ("x", "h"))
    sums = lax.psum(sums, "y")
    ds = ds[:rows] + dc
    count = 1.0 * lax.axis_size(REP) * batch * batch
    s = jnp.sum(sums, axis=1) / count
    return ds[None], do[None], s[0], s[1], s[2]


def solution(mesh):
    axes = Mesh(mesh.devices.reshape(NY, NX, NC, NZ, NH), BLK + REP)
    split_of = P(REP, BLK, None)
    in_specs = (split_of, split_of, P(REP, None), P(), P())
    out_specs = (split_of, split_of, P(), P(), P())
    return jax.shard_map(local, mesh=axes, in_specs=in_specs, out_specs=out_specs, check_vma=False)
```

time: 228 us -> 136 us (0.60)
  waiting for transfers between devices: 81.9 us -> 6.8 us
  blocking collectives: 98.3 us -> 45.7 us
  starting transfers between devices: 0.08 us -> 43.5 us
  matrix products: 25.9 us -> 0 us
  Pallas kernels: 0 us -> 15.7 us
  other arithmetic: 0.01 us -> 6.37 us
  between operations: 20.7 us -> 15.7 us
    all_gather x2 -> x0, waiting for transfers between devices: 80.5 us -> none  [the longest x1 80.5 us: local(): lax.all_gather(result_embeds, 'blk', axis=1, tiled=True)[0]]
    psum x1 -> x4, blocking collectives: 98.3 us -> 45.7 us  [the longest x1 15.3 us: local(): sums = lax.psum(sums, 'z')]
    ppermute x0 -> x11, starting transfers between devices: none -> 43.5 us  [local(): send = lambda a, p: lax.ppermute(a, BLK, p)]
    dot_general x3 -> x0, matrix products: 25.9 us -> none  [the longest x1 12 us: local(): lax.dot_general(multiplier, submatrix_piece, (((0,), (0,)), ((), ())), pr...]
    pallas_call x0 -> x4, Pallas kernels: none -> 15.7 us  [pairs(): pl.pallas_call(functools.partial(pair_kernel, 1.0 / math.sqrt(d), not car...]
    ppermute x0 -> x11, waiting for transfers between devices: none -> 3.64 us  [local(): send = lambda a, p: lax.ppermute(a, BLK, p)]
    reduce_scatter x0 -> x1, waiting for transfers between devices: none -> 3.14 us  [local(): do = lax.psum_scatter(do, 'y', scatter_dimension=0, tiled=True)]
  transfers between devices with their start and end apart: 2 -> 12, of which waited for: 1 -> 4; matrix products, arithmetic and copies ran while one was open for 6% -> 4% of each run, Pallas kernels for 0% -> 10%
where the time goes in v1:
time: 136 us; the launch traced here: 135 us
  blocking collectives  45.7 us (34%)
  starting transfers between devices  43.5 us (32%)
  Pallas kernels  15.7 us (12%)
  between operations  15.7 us (12%)
  waiting for transfers between devices  6.8 us (5%)
  other arithmetic  6.37 us (5%)
  local copies, waits for them, and re-layouts  1.5 us (1%)
    ppermute x11, starting transfers between devices, local(): send = lambda a, p: lax.ppermute(a, BLK, p)  43.5 us
    pallas_call x4, Pallas kernels, pairs(): pl.pallas_call(functools.partial(pair_kernel, 1.0 / math.sqrt(d), not car...  15.7 us
    psum x1, blocking collectives, local(): sums = lax.psum(sums, 'z')  15.3 us
    psum x1, blocking collectives, local(): sums = lax.psum(sums, 'y')  15.2 us
    psum x1, blocking collectives, local(): sums = lax.psum(sums, ('x', 'h'))  9.32 us
    psum x1, blocking collectives, local(): sums = lax.psum(sums, 'c')  5.87 us
    ppermute x11, waiting for transfers between devices, local(): send = lambda a, p: lax.ppermute(a, BLK, p)  3.64 us
    reduce_scatter x1, waiting for transfers between devices, local(): do = lax.psum_scatter(do, 'y', scatter_dimension=0, tiled=True)  3.14 us
  transfers between devices with their start and end apart: 12, of which 4 were waited for; matrix products, arithmetic and copies ran while one was open for 4% of the time, Pallas kernels for 10%

profile of v1, /device:TPU:1, one launch (start us, length us, event | category | flops | bytes accessed | tf_op | source)
XLA Modules:
  0.0 135.2 jit_solution(3562791554854940356)
XLA Ops:
  7.2 0.0 reduce-scatter.2.cloned.1.call-start
  7.2 8.8 %collective-permute-start = (bf16[128,1024]{1,0:T(8,128)(2,1)}, bf16[128,1024]{1,0:T(8,128)(2,1)S(1)}, u32[]{:S(2)}, u32[]{:S(2)}) collective-permute-start(bf16[128,1024]{1,0:T(8,128)(2,1)} %bitcast.38), channel_id=1, source_target_pairs={{0,16},{16,0},{32,48},{48,32},{64,80},{80,64},{96,112},{112,96},{1... | collective-permute-start | bytes 786440 | tf_op jit(solution)/shard_map/ppermute | solution.py:136
  16.0 1.4 collective-permute-done
  17.4 1.0 pad_maximum_fusion.1
  18.3 1.9 %collective-permute-start.1 = (bf16[256,1024]{1,0:T(8,128)(2,1)S(1)}, bf16[256,1024]{1,0:T(8,128)(2,1)S(1)}, u32[]{:S(2)}, u32[]{:S(2)}) collective-permute-start(bf16[256,1024]{1,0:T(8,128)(2,1)S(1)} %pad_maximum_fusion.1), channel_id=1, source_target_pairs={{0,32},{16,48},{32,0},{48,16},{64,96},{80,112},{96,64},{112,80},{1... | collective-permute-start | bytes 1572872 | tf_op jit(solution)/shard_map/ppermute | solution.py:136
  20.3 1.9 %collective-permute-start.2 = (bf16[128,1024]{1,0:T(8,128)(2,1)}, bf16[128,1024]{1,0:T(8,128)(2,1)}, u32[]{:S(2)}, u32[]{:S(2)}) collective-permute-start(bf16[128,1024]{1,0:T(8,128)(2,1)} %bitcast.35), channel_id=1, source_target_pairs={{0,64},{16,80},{32,96},{48,112},{64,128},{80,144},{96,160},{112,17... | collective-permute-start | bytes 786440 | tf_op jit(solution)/shard_map/ppermute | solution.py:136
  22.2 4.6 %collective-permute-start.4 = (bf16[128,1024]{1,0:T(8,128)(2,1)}, bf16[128,1024]{1,0:T(8,128)(2,1)}, u32[]{:S(2)}, u32[]{:S(2)}) collective-permute-start(bf16[128,1024]{1,0:T(8,128)(2,1)} %bitcast.36), channel_id=1, source_target_pairs={{0,448},{16,464},{32,480},{48,496},{64,0},{80,16},{96,32},{112,48}... | collective-permute-start | bytes 786440 | tf_op jit(solution)/shard_map/ppermute | solution.py:136
  26.9 0.1 add_multiply_fusion.2
  28.3 0.0 copy-start
  28.3 0.8 fusion.1
  29.1 2.2 %collective-permute-done.2.rest_1_ = bf16[128,1024]{1,0:T(8,128)(2,1)} collective-permute-done((bf16[128,1024]{1,0:T(8,128)(2,1)}, bf16[128,1024]{1,0:T(8,128)(2,1)}, u32[]{:S(2)}, u32[]{:S(2)}) %collective-permute-start.2) | collective-permute-done | bytes 262176 | tf_op jit(solution)/shard_map/ppermute | solution.py:136
  31.2 1.9 %collective-permute-start.3 = (bf16[128,1024]{1,0:T(8,128)(2,1)}, bf16[128,1024]{1,0:T(8,128)(2,1)}, u32[]{:S(2)}, u32[]{:S(2)}) collective-permute-start(bf16[128,1024]{1,0:T(8,128)(2,1)} %collective-permute-done.2.rest_1_), channel_id=1, source_target_pairs={{0,64},{16,80},{32,96},{48,112},{64,128},{80,144},{96,160},{112,17... | collective-permute-start | bytes 786440 | tf_op jit(solution)/shard_map/ppermute | solution.py:136
  33.1 0.0 collective-permute-done.4.rest_2_
  33.1 4.6 %collective-permute-start.5 = (bf16[128,1024]{1,0:T(8,128)(2,1)}, bf16[128,1024]{1,0:T(8,128)(2,1)}, u32[]{:S(2)}, u32[]{:S(2)}) collective-permute-start(bf16[128,1024]{1,0:T(8,128)(2,1)} %collective-permute-done.4.rest_2_), channel_id=1, source_target_pairs={{0,448},{16,464},{32,480},{48,496},{64,0},{80,16},{96,32},{112,48}... | collective-permute-start | bytes 786440 | tf_op jit(solution)/shard_map/ppermute | solution.py:136
  37.7 0.1 pad_maximum_fusion.2.scal_ref
  37.8 0.0 collective-permute-done.1
  37.8 1.0 pad_maximum_fusion.v_ref
  38.8 0.0 copy-done
  38.8 5.0 %shard_map.92 = (f32[512,1024]{1,0:T(8,128)S(1)}, f32[3,128]{1,0:T(4,128)S(1)}, f32[1024,1024]{1,0:T(8,128)}) custom-call(s32[3]{0:T(128)S(1)} %get-tuple-element.57.base_ref, s32[3]{0:T(128)S(1)} %get-tuple-element.58.to_ref, f32[2]{0:T(128)S(1)} %pad_maximum_fusion.2.scal_ref, s32[1,512]{1,0:T(1,128)S(1)} %bitcast.31, ...), custom_call_target="tpu_custom_call" | custom-call | flops 1207959552 | bytes 7602176 | tf_op jit(solution)/shard_map/pallas_call | solution.py:104
  43.9 0.0 collective-permute-done.3.rest_0_
  43.9 0.0 collective-permute-done.5.rest_1_
  43.9 1.9 %collective-permute-start.6 = (bf16[128,1024]{1,0:T(8,128)(2,1)}, bf16[128,1024]{1,0:T(8,128)(2,1)S(1)}, u32[]{:S(2)}, u32[]{:S(2)}) collective-permute-start(bf16[128,1024]{1,0:T(8,128)(2,1)} %collective-permute-done.3.rest_0_), channel_id=1, source_target_pairs={{0,64},{16,80},{32,96},{48,112},{64,128},{80,144},{96,160},{112,17... | collective-permute-start | bytes 786440 | tf_op jit(solution)/shard_map/ppermute | solution.py:136
  45.8 4.6 %collective-permute-start.7 = (bf16[128,1024]{1,0:T(8,128)(2,1)}, bf16[128,1024]{1,0:T(8,128)(2,1)}, u32[]{:S(2)}, u32[]{:S(2)}) collective-permute-start(bf16[128,1024]{1,0:T(8,128)(2,1)} %collective-permute-done.5.rest_1_), channel_id=1, source_target_pairs={{0,448},{16,464},{32,480},{48,496},{64,0},{80,16},{96,32},{112,48}... | collective-permute-start | bytes 786440 | tf_op jit(solution)/shard_map/ppermute | solution.py:136
  50.4 0.1 add_multiply_fusion.1
  50.5 4.0 %shard_map.93 = (f32[512,1024]{1,0:T(8,128)S(1)}, f32[3,128]{1,0:T(4,128)S(1)}, f32[1024,1024]{1,0:T(8,128)}) custom-call(s32[2]{0:T(128)S(1)} %get-tuple-element.55.base_ref, s32[2]{0:T(128)S(1)} %get-tuple-element.56.to_ref, f32[2]{0:T(128)S(1)} %pad_maximum_fusion.2.scal_ref, ...), custom_call_target="tpu_custom_call", output_to_operand_aliasing={{0}: (7, {}), {1}: (8, {}), {2}: (9, {})} | custom-call | flops 805306368 | bytes 6815744 | tf_op jit(solution)/shard_map/pallas_call | solution.py:104
  54.5 0.0 collective-permute-done.6.rest_0_
  54.5 0.0 collective-permute-done.7.rest_1_
  54.5 1.7 %broadcast_select_fusion = bf16[128,1024]{1,0:T(8,128)(2,1)} fusion(bf16[128,1024]{1,0:T(8,128)(2,1)S(1)} %collective-permute-done.6.rest_0_, bf16[128,1024]{1,0:T(8,128)(2,1)} %collective-permute-done.7.rest_1_, pred[]{:T(512)S(6)} %eq.26), kind=kLoop, calls=%fused_computation.5 | loop fusion | flops 131072 | bytes 786433 | tf_op jit(solution)/shard_map/jit(_where)/select_n | solution.py:163
  56.2 5.0 %collective-permute-start.8 = (bf16[128,1024]{1,0:T(8,128)(2,1)}, bf16[128,1024]{1,0:T(8,128)(2,1)}, u32[]{:S(2)}, u32[]{:S(2)}) collective-permute-start(bf16[128,1024]{1,0:T(8,128)(2,1)} %broadcast_select_fusion), channel_id=1, source_target_pairs={{0,64},{16,464},{32,96},{48,496},{64,128},{80,16},{96,160},{112,48... | collective-permute-start | bytes 786440 | tf_op jit(solution)/shard_map/ppermute | solution.py:136
  61.3 0.1 add_multiply_fusion
  61.4 3.9 %shard_map.94 = (f32[512,1024]{1,0:T(8,128)S(1)}, f32[3,128]{1,0:T(4,128)S(1)}, f32[1024,1024]{1,0:T(8,128)}) custom-call(s32[2]{0:T(128)S(1)} %get-tuple-element.53.base_ref, s32[2]{0:T(128)S(1)} %get-tuple-element.54.to_ref, f32[2]{0:T(128)S(1)} %pad_maximum_fusion.2.scal_ref, ...), custom_call_target="tpu_custom_call", output_to_operand_aliasing={{0}: (7, {}), {1}: (8, {}), {2}: (9, {})} | custom-call | flops 805306368 | bytes 6815744 | tf_op jit(solution)/shard_map/pallas_call | solution.py:104
  65.3 0.0 collective-permute-done.8.rest_0_
  65.3 2.8 %shard_map.95 = (f32[512,1024]{1,0:T(8,128)S(1)}, f32[3,128]{1,0:T(4,128)S(1)}, f32[1024,1024]{1,0:T(8,128)}) custom-call(s32[1]{0:T(128)S(6)} %mul.70.base_ref, s32[1]{0:T(128)} %bitcast.to_ref, f32[2]{0:T(128)S(1)} %pad_maximum_fusion.2.scal_ref, s32[1,512]{1,0:T(1,128)S(1)} %bitcast.34, ...), custom_call_target="tpu_custom_call", output_to_operand_aliasing={{0}: (6, {}), {1}: (7, {}), {2}: (8, {})} | custom-call | flops 402653184 | bytes 6029312 | tf_op jit(solution)/shard_map/pallas_call | solution.py:104
  68.1 0.0 reduce-scatter.2.cloned.1.call-update
  68.1 0.1 slice.22
  68.2 2.5 %collective-permute-start.9 = (f32[256,1024]{1,0:T(8,128)S(1)}, f32[256,1024]{1,0:T(8,128)}, u32[]{:S(2)}, u32[]{:S(2)}) collective-permute-start(f32[256,1024]{1,0:T(8,128)S(1)} %slice.22), channel_id=1, source_target_pairs={{0,32},{16,48},{32,0},{48,16},{64,96},{80,112},{96,64},{112,80},{1... | collective-permute-start | bytes 3145736 | tf_op jit(solution)/shard_map/ppermute | solution.py:136
  70.7 5.9 %psum.28 = f32[3,128]{1,0:T(4,128)S(1)} all-reduce(f32[3,128]{1,0:T(4,128)S(1)} %get-tuple-element.49), channel_id=1, replica_groups=mesh['y'=8,'x'=2,'c'=2,'z'=8,'h'=2] {'c'}, use_global_device_ids=true, to_apply=%region_0.1 | all-reduce | flops 384 | bytes 3072 | tf_op jit(solution)/shard_map/psum | solution.py:169
  76.6 15.3 %psum.29 = f32[3,128]{1,0:T(4,128)S(1)} all-reduce(f32[3,128]{1,0:T(4,128)S(1)} %psum.28), channel_id=1, replica_groups=mesh['y'=8,'x'=2,'c'=2,'z'=8,'h'=2] {'z'}, use_global_device_ids=true, to_apply=%region_1.2 | all-reduce | flops 384 | bytes 3072 | tf_op jit(solution)/shard_map/psum | solution.py:170
  91.9 0.1 collective-permute-done.9
  92.0 1.4 %slice_add_fusion = f32[256,1024]{1,0:T(8,128)S(1)} fusion(f32[256,1024]{1,0:T(8,128)} %collective-permute-done.9, f32[512,1024]{1,0:T(8,128)S(1)} %get-tuple-element.48), kind=kLoop, calls=%fused_computation.1 | loop fusion | flops 262144 | bytes 3145728 | tf_op jit(solution)/shard_map/add | solution.py:172
  93.4 5.8 %collective-permute-start.10 = (f32[128,1024]{1,0:T(8,128)S(1)}, f32[128,1024]{1,0:T(8,128)S(1)}, u32[]{:S(2)}, u32[]{:S(2)}) collective-permute-start(f32[128,1024]{1,0:T(8,128)S(1)} %slice.29), channel_id=1, source_target_pairs={{0,16},{16,0},{32,48},{48,32},{64,80},{80,64},{96,112},{112,96},{1... | collective-permute-start | bytes 1572872 | tf_op jit(solution)/shard_map/ppermute | solution.py:136
  99.1 9.3 %psum.30 = f32[3,128]{1,0:T(4,128)S(1)} all-reduce(f32[3,128]{1,0:T(4,128)S(1)} %psum.29), channel_id=1, replica_groups=mesh['y'=8,'x'=2,'c'=2,'z'=8,'h'=2] {'x','h'}, use_global_device_ids=true, to_apply=%region_3.4 | all-reduce | flops 384 | bytes 3072 | tf_op jit(solution)/shard_map/psum | solution.py:174
  108.5 15.2 %psum.31 = f32[3,128]{1,0:T(4,128)S(1)} all-reduce(f32[3,128]{1,0:T(4,128)S(1)} %psum.30), channel_id=1, replica_groups=mesh['y'=8,'x'=2,'c'=2,'z'=8,'h'=2] {'y'}, use_global_device_ids=true, to_apply=%region_4.5 | all-reduce | flops 384 | bytes 3072 | tf_op jit(solution)/shard_map/psum | solution.py:175
  123.7 0.1 reduce_sum.9
  123.8 0.6 fusion.5
  124.4 0.0 collective-permute-done.10
  124.4 0.9 fusion
  125.2 3.1 %reduce-scatter.2.cloned.1.call-done = f32[128,1024]{1,0:T(8,128)} async-done(((f32[1024,1024]{1,0:T(8,128)}), f32[128,1024]{1,0:T(8,128)}) %reduce-scatter.2.cloned.1.call-update) | async-done | bytes 524304 | tf_op jit(solution)/shard_map/reduce_scatter | solution.py:167
  (3 shorter events, 0.1 us)
Async XLA Ops:
  7.2 121.2 %reduce-scatter.2.cloned.1.call-start = ((), (), s32[]{:S(2)}) async-start(), calls=%async_computation.1 | async-start | bytes 4718592 | tf_op jit(solution)/shard_map/reduce_scatter | solution.py:167
  7.2 10.1 %collective-permute-start = (bf16[128,1024]{1,0:T(8,128)(2,1)}, bf16[128,1024]{1,0:T(8,128)(2,1)S(1)}, u32[]{:S(2)}, u32[]{:S(2)}) collective-permute-start(bf16[128,1024]{1,0:T(8,128)(2,1)} %bitcast.38), channel_id=1, source_target_pairs={{0,16},{16,0},{32,48},{48,32},{64,80},{80,64},{96,112},{112,96},{1... | collective-permute-start | bytes 786440 | tf_op jit(solution)/shard_map/ppermute | solution.py:136
  18.3 19.5 %collective-permute-start.1 = (bf16[256,1024]{1,0:T(8,128)(2,1)S(1)}, bf16[256,1024]{1,0:T(8,128)(2,1)S(1)}, u32[]{:S(2)}, u32[]{:S(2)}) collective-permute-start(bf16[256,1024]{1,0:T(8,128)(2,1)S(1)} %pad_maximum_fusion.1), channel_id=1, source_target_pairs={{0,32},{16,48},{32,0},{48,16},{64,96},{80,112},{96,64},{112,80},{1... | collective-permute-start | bytes 1572872 | tf_op jit(solution)/shard_map/ppermute | solution.py:136
  20.3 10.9 %collective-permute-start.2 = (bf16[128,1024]{1,0:T(8,128)(2,1)}, bf16[128,1024]{1,0:T(8,128)(2,1)}, u32[]{:S(2)}, u32[]{:S(2)}) collective-permute-start(bf16[128,1024]{1,0:T(8,128)(2,1)} %bitcast.35), channel_id=1, source_target_pairs={{0,64},{16,80},{32,96},{48,112},{64,128},{80,144},{96,160},{112,17... | collective-permute-start | bytes 786440 | tf_op jit(solution)/shard_map/ppermute | solution.py:136
  22.2 10.9 %collective-permute-start.4 = (bf16[128,1024]{1,0:T(8,128)(2,1)}, bf16[128,1024]{1,0:T(8,128)(2,1)}, u32[]{:S(2)}, u32[]{:S(2)}) collective-permute-start(bf16[128,1024]{1,0:T(8,128)(2,1)} %bitcast.36), channel_id=1, source_target_pairs={{0,448},{16,464},{32,480},{48,496},{64,0},{80,16},{96,32},{112,48}... | collective-permute-start | bytes 786440 | tf_op jit(solution)/shard_map/ppermute | solution.py:136
  28.3 10.6 %copy-start = (bf16[1,128,1024]{2,1,0:T(8,128)(2,1)S(1)}, bf16[1,128,1024]{2,1,0:T(8,128)(2,1)}, u32[]{:S(2)}) copy-start(bf16[1,128,1024]{2,1,0:T(8,128)(2,1)} %param.6) | copy-start | bytes 786436
  31.2 12.7 %collective-permute-start.3 = (bf16[128,1024]{1,0:T(8,128)(2,1)}, bf16[128,1024]{1,0:T(8,128)(2,1)}, u32[]{:S(2)}, u32[]{:S(2)}) collective-permute-start(bf16[128,1024]{1,0:T(8,128)(2,1)} %collective-permute-done.2.rest_1_), channel_id=1, source_target_pairs={{0,64},{16,80},{32,96},{48,112},{64,128},{80,144},{96,160},{112,17... | collective-permute-start | bytes 786440 | tf_op jit(solution)/shard_map/ppermute | solution.py:136
  33.1 10.7 %collective-permute-start.5 = (bf16[128,1024]{1,0:T(8,128)(2,1)}, bf16[128,1024]{1,0:T(8,128)(2,1)}, u32[]{:S(2)}, u32[]{:S(2)}) collective-permute-start(bf16[128,1024]{1,0:T(8,128)(2,1)} %collective-permute-done.4.rest_2_), channel_id=1, source_target_pairs={{0,448},{16,464},{32,480},{48,496},{64,0},{80,16},{96,32},{112,48}... | collective-permute-start | bytes 786440 | tf_op jit(solution)/shard_map/ppermute | solution.py:136
  43.9 10.6 %collective-permute-start.6 = (bf16[128,1024]{1,0:T(8,128)(2,1)}, bf16[128,1024]{1,0:T(8,128)(2,1)S(1)}, u32[]{:S(2)}, u32[]{:S(2)}) collective-permute-start(bf16[128,1024]{1,0:T(8,128)(2,1)} %collective-permute-done.3.rest_0_), channel_id=1, source_target_pairs={{0,64},{16,80},{32,96},{48,112},{64,128},{80,144},{96,160},{112,17... | collective-permute-start | bytes 786440 | tf_op jit(solution)/shard_map/ppermute | solution.py:136
  45.8 8.7 %collective-permute-start.7 = (bf16[128,1024]{1,0:T(8,128)(2,1)}, bf16[128,1024]{1,0:T(8,128)(2,1)}, u32[]{:S(2)}, u32[]{:S(2)}) collective-permute-start(bf16[128,1024]{1,0:T(8,128)(2,1)} %collective-permute-done.5.rest_1_), channel_id=1, source_target_pairs={{0,448},{16,464},{32,480},{48,496},{64,0},{80,16},{96,32},{112,48}... | collective-permute-start | bytes 786440 | tf_op jit(solution)/shard_map/ppermute | solution.py:136
  56.2 9.1 %collective-permute-start.8 = (bf16[128,1024]{1,0:T(8,128)(2,1)}, bf16[128,1024]{1,0:T(8,128)(2,1)}, u32[]{:S(2)}, u32[]{:S(2)}) collective-permute-start(bf16[128,1024]{1,0:T(8,128)(2,1)} %broadcast_select_fusion), channel_id=1, source_target_pairs={{0,64},{16,464},{32,96},{48,496},{64,128},{80,16},{96,160},{112,48... | collective-permute-start | bytes 786440 | tf_op jit(solution)/shard_map/ppermute | solution.py:136
  68.2 23.7 %collective-permute-start.9 = (f32[256,1024]{1,0:T(8,128)S(1)}, f32[256,1024]{1,0:T(8,128)}, u32[]{:S(2)}, u32[]{:S(2)}) collective-permute-start(f32[256,1024]{1,0:T(8,128)S(1)} %slice.22), channel_id=1, source_target_pairs={{0,32},{16,48},{32,0},{48,16},{64,96},{80,112},{96,64},{112,80},{1... | collective-permute-start | bytes 3145736 | tf_op jit(solution)/shard_map/ppermute | solution.py:136
  93.4 31.0 %collective-permute-start.10 = (f32[128,1024]{1,0:T(8,128)S(1)}, f32[128,1024]{1,0:T(8,128)S(1)}, u32[]{:S(2)}, u32[]{:S(2)}) collective-permute-start(f32[128,1024]{1,0:T(8,128)S(1)} %slice.29), channel_id=1, source_target_pairs={{0,16},{16,0},{32,48},{48,32},{64,80},{80,64},{96,112},{112,96},{1... | collective-permute-start | bytes 1572872 | tf_op jit(solution)/shard_map/ppermute | solution.py:136
Sparse Core Ops, SparseCore 0:
  68.2 60.1 reduce-scatter.1

commit v2 on v1

v2 whole, which is shorter than its diff:
```python
import functools
import math

import jax
import jax.numpy as jnp
from jax import lax
from jax.experimental import pallas as pl
from jax.experimental.pallas import tpu as pltpu
from jax.sharding import Mesh
from jax.sharding import PartitionSpec as P

NY, NX, NC, NZ, NH = 8, 2, 2, 8, 2
BLK, REP = ("y", "x", "c"), ("z", "h")


def at(y, x, c):
    return (y % NY) * NX * NC + (x % NX) * NC + (c % NC)


def move(dy=0, dx=0, dc=0):
    return [
        (at(y, x, c), at(y + dy, x + dx, c + dc))
        for y in range(NY)
        for x in range(NX)
        for c in range(NC)
    ]


def split(step):
    return [
        (at(y, x, c), at(y + (step if c == 0 else -step), x, c))
        for y in range(NY)
        for x in range(NX)
        for c in range(NC)
    ]


def pair_kernel(unit, first, groups, base_ref, to_ref, scal_ref, idx_ref, *rest):
    n = sum(groups)
    v_hbm, r_hbm, rest = rest[:2], rest[2 : 2 + n], rest[2 + n :]
    if not first:
        ds_in, sums_in, _, *rest = rest
    ds_ref, sums_ref, do_ref, v_ref, held, out_sems = rest
    half = v_hbm[0].shape[0]
    width = r_hbm[0].shape[0]
    m = 2 * half
    stretch = scal_ref[0]
    offset = scal_ref[1]
    scale = stretch * unit
    matched = idx_ref[...]
    sums = [jnp.zeros((8, m), jnp.float32) for _ in range(3)]
    for i in range(2):
        v_ref[i * half : (i + 1) * half, :] = v_hbm[i][...]
    v = v_ref[...]
    stores = {}
    k = 0
    for g, size in enumerate(groups):
        slot = g % 2
        for store in stores.pop(slot, []):
            store.wait()
        r = jnp.concatenate([r_hbm[k + i][...] for i in range(size)], axis=0)
        y = (
            lax.dot_general(r, v, (((1,), (1,)), ((), ())), preferred_element_type=jnp.float32)
            * unit
        )
        x = stretch * y + offset
        lane = lax.broadcasted_iota(jnp.int32, (width, m), 0)
        hit = jnp.concatenate([base_ref[k + i] + lane == matched for i in range(size)], axis=0)
        t = jnp.where(hit, -x, x)
        e = jnp.exp(-jnp.abs(t))
        inv = 1.0 / (1.0 + e)
        sig = jnp.where(t >= 0, inv, e * inv)
        grad = jnp.where(hit, -sig, sig)
        for i, a in enumerate((jnp.maximum(t, 0.0) + jnp.log1p(e), grad * y, grad)):
            sums[i] += jnp.sum(a.reshape(size * width // 8, 8, m), axis=0)
        coef = (grad * scale).astype(jnp.bfloat16)
        held[slot, : size * width, :] = jnp.dot(coef, v, preferred_element_type=jnp.float32)
        stores[slot] = []
        for i in range(size):
            rows = pl.ds(pl.multiple_of(to_ref[k + i] * width, width), width)
            stores[slot].append(
                pltpu.make_async_copy(
                    held.at[slot, pl.ds(i * width, width)], do_ref.at[rows], out_sems.at[slot, i]
                )
            )
            stores[slot][i].start()
        part = lax.dot_general(
            coef, r, (((0,), (0,)), ((), ())), preferred_element_type=jnp.float32
        )
        if g:
            ds_ref[...] += part
        elif first:
            ds_ref[...] = part
        else:
            ds_ref[...] = ds_in[...] + part
        k += size
    for i, a in enumerate(sums):
        s = a[:, :128]
        for j in range(128, m, 128):
            s += a[:, j : j + 128]
        s = jnp.sum(s, axis=0, keepdims=True)
        sums_ref[i : i + 1, :] = s if first else s + sums_in[i : i + 1, :]
    for slot in sorted(stores):
        for store in stores[slot]:
            store.wait()


def pairs(base, to, scal, idx, vs, rs, groups, carry=()):
    half, d = vs[0].shape
    m = 2 * half
    width = rs[0].shape[0]
    n = len(rs)
    cols = n * width
    vm = pl.BlockSpec(memory_space=pltpu.VMEM)
    sm = pl.BlockSpec(memory_space=pltpu.SMEM)
    hbm = pl.BlockSpec(memory_space=pltpu.HBM)
    args = [base, to, scal, idx, *vs, *rs, *carry]
    first = len(args) - 3
    return pl.pallas_call(
        functools.partial(pair_kernel, 1.0 / math.sqrt(d), not carry, groups),
        out_shape=[
            jax.ShapeDtypeStruct((m, d), jnp.float32),
            jax.ShapeDtypeStruct((3, 128), jnp.float32),
            jax.ShapeDtypeStruct((NY * width, d), jnp.float32),
        ],
        in_specs=[sm, sm, sm, vm] + [vm] * (2 + n) + ([vm, vm, hbm] if carry else []),
        out_specs=[vm, vm, hbm],
        scratch_shapes=[
            pltpu.VMEM((m, d), jnp.bfloat16),
            pltpu.VMEM((2, max(groups) * width, d), jnp.float32),
            pltpu.SemaphoreType.DMA((2, max(groups))),
        ],
        input_output_aliases={first + i: i for i in range(3)} if carry else {},
        compiler_params=pltpu.CompilerParams(vmem_limit_bytes=48 * 1024 * 1024),
        cost_estimate=pl.CostEstimate(
            flops=6 * m * cols * d,
            bytes_accessed=2 * (m + cols) * d + 4 * (2 * m + cols) * d,
            transcendentals=3 * m * cols,
        ),
    )(*args)


def local(visit_embeds, result_embeds, matched_result_index, logit_stretch, logit_offset):
    v0 = visit_embeds[0]
    r0 = result_embeds[0]
    rows = v0.shape[0]
    index = matched_result_index[0]
    batch = index.shape[0]
    me = lax.axis_index(BLK)
    y, x, c = me // (NX * NC), (me // NC) % NX, me % NC
    tie = lambda *xs: lax.optimization_barrier(xs)
    send = lambda a, p: lax.ppermute(a, BLK, p)
    with_a, with_b = split(1), split(-1)
    side = 2 * c - 1

    a1, b1 = send(r0, with_a), send(r0, with_b)
    own = jnp.concatenate([v0, send(v0, move(dc=1))], axis=0)
    vs = (own, send(own, move(dx=1)))
    a2, b2 = send(a1, with_a), send(b1, with_b)
    a3, b3 = send(a2, with_a), send(b2, with_b)

    scal = jnp.stack([logit_stretch, logit_offset])
    idx = jnp.concatenate(
        [
            lax.dynamic_slice_in_dim(index, at(y, x + a, c + o) * rows, rows)
            for a in (0, 1)
            for o in (0, 1)
        ]
    )[None]

    def work(steps, rs, groups, carry=()):
        to = jnp.stack([(y + side * k) % NY for k in steps]).astype(jnp.int32)
        base = (to * (NX * NC) + x * NC + c) * rows
        return pairs(base.astype(jnp.int32), to, scal, idx, vs, rs, groups, carry)

    carry = work((0, 1, -1, 2, -2), (r0, a1, b1, a2, b2), (1, 2, 2))
    a3, b3, *carry = tie(a3, b3, *carry)
    a4 = send(a3, with_a)
    carry = work((3, -3), (a3, b3), (2,), carry)
    ds, sums, do = work((4,), (a4,), (1,), carry)

    do = lax.psum_scatter(do, "y", scatter_dimension=0, tiled=True)
    dx = send(ds[2 * rows :], move(dx=1))
    sums = lax.psum(sums, "c")
    sums = lax.psum(sums, "z")
    sums = lax.psum(sums, ("x", "h"))
    sums, dx = tie(sums, dx)
    ds = ds[: 2 * rows] + dx
    dc = send(ds[rows:], move(dc=1))
    sums = lax.psum(sums, "y")
    ds = ds[:rows] + dc
    count = 1.0 * lax.axis_size(REP) * batch * batch
    s = jnp.sum(sums, axis=1) / count
    return ds[None], do[None], s[0], s[1], s[2]


def solution(mesh):
    axes = Mesh(mesh.devices.reshape(NY, NX, NC, NZ, NH), BLK + REP)
    split_of = P(REP, BLK, None)
    in_specs = (split_of, split_of, P(REP, None), P(), P())
    out_specs = (split_of, split_of, P(), P(), P())
    return jax.shard_map(local, mesh=axes, in_specs=in_specs, out_specs=out_specs, check_vma=False)
```

time: 136 us -> 129 us (0.949)
  waiting for transfers between devices: 6.8 us -> 2.34 us
  local copies, waits for them, and re-layouts: 1.5 us -> 5.79 us
  Pallas kernels: 15.7 us -> 12.3 us
  other arithmetic: 6.37 us -> 3.53 us
  starting transfers between devices: 43.5 us -> 41.6 us
  blocking collectives: 45.7 us -> 47.4 us
    unnamed x2 -> x10, local copies, waits for them, and re-layouts: 0.01 us -> 4.25 us
    psum x1, blocking collectives: 15.3 us -> 19.5 us  [local(): sums = lax.psum(sums, 'z')]
    pallas_call x4 -> x3, Pallas kernels: 15.7 us -> 12.3 us  [pairs(): pl.pallas_call(functools.partial(pair_kernel, 1.0 / math.sqrt(d), not car...]
    reduce_scatter x1, waiting for transfers between devices: 3.14 us -> 0.01 us  [local(): do = lax.psum_scatter(do, 'y', scatter_dimension=0, tiled=True)]
    psum x1, blocking collectives: 5.87 us -> 3.57 us  [local(): sums = lax.psum(sums, 'c')]
    ppermute x11, starting transfers between devices: 43.5 us -> 41.5 us  [local(): send = lambda a, p: lax.ppermute(a, BLK, p)]
    select_n x1 -> x0, other arithmetic: 1.69 us -> none  [local(): r4 = send(jnp.where(c == 0, l3, u3), split(1))]
  transfers between devices with their start and end apart: 12 -> 12, of which waited for: 4 -> 1; matrix products, arithmetic and copies ran while one was open for 4% -> 4% of each run, Pallas kernels for 10% -> 7%
where the time goes in v2:
time: 129 us
  blocking collectives  47.4 us (37%)
  starting transfers between devices  41.6 us (32%)
  between operations  15.7 us (12%)
  Pallas kernels  12.3 us (10%)
  local copies, waits for them, and re-layouts  5.79 us (4%)
  other arithmetic  3.53 us (3%)
  waiting for transfers between devices  2.34 us (2%)
    ppermute x11, starting transfers between devices, local(): send = lambda a, p: lax.ppermute(a, BLK, p)  41.5 us
    psum x1, blocking collectives, local(): sums = lax.psum(sums, 'z')  19.5 us
    psum x1, blocking collectives, local(): sums = lax.psum(sums, 'y')  14.8 us
    pallas_call x3, Pallas kernels, pairs(): pl.pallas_call(functools.partial(pair_kernel, 1.0 / math.sqrt(d), not car...  12.3 us
    psum x1, blocking collectives, local(): sums = lax.psum(sums, ('x', 'h'))  9.53 us
    unnamed x10, local copies, waits for them, and re-layouts  4.25 us
    psum x1, blocking collectives, local(): sums = lax.psum(sums, 'c')  3.57 us
  transfers between devices with their start and end apart: 12, of which 1 were waited for; matrix products, arithmetic and copies ran while one was open for 4% of the time, Pallas kernels for 7%

profile of v2, /device:TPU:1, one launch (start us, length us, event | category | flops | bytes accessed | tf_op | source)
XLA Modules:
  0.0 128.7 jit_solution(9738899462266049051)
XLA Ops:
  7.2 0.0 reduce-scatter.2.cloned.1.call-start
  7.2 8.8 %collective-permute-start = (bf16[128,1024]{1,0:T(8,128)(2,1)}, bf16[128,1024]{1,0:T(8,128)(2,1)S(1)}, u32[]{:S(2)}, u32[]{:S(2)}) collective-permute-start(bf16[128,1024]{1,0:T(8,128)(2,1)} %bitcast.37), channel_id=1, source_target_pairs={{0,16},{16,0},{32,48},{48,32},{64,80},{80,64},{96,112},{112,96},{1... | collective-permute-start | bytes 786440 | tf_op jit(solution)/shard_map/ppermute | solution.py:152
  16.0 1.9 %collective-permute-start.5 = (bf16[128,1024]{1,0:T(8,128)(2,1)}, bf16[128,1024]{1,0:T(8,128)(2,1)S(1)}, u32[]{:S(2)}, u32[]{:S(2)}) collective-permute-start(bf16[128,1024]{1,0:T(8,128)(2,1)} %bitcast.34), channel_id=1, source_target_pairs={{0,448},{16,80},{32,480},{48,112},{64,0},{80,144},{96,32},{112,176... | collective-permute-start | bytes 786440 | tf_op jit(solution)/shard_map/ppermute | solution.py:152
  17.9 4.6 %collective-permute-start.2 = (bf16[128,1024]{1,0:T(8,128)(2,1)}, bf16[128,1024]{1,0:T(8,128)(2,1)S(1)}, u32[]{:S(2)}, u32[]{:S(2)}) collective-permute-start(bf16[128,1024]{1,0:T(8,128)(2,1)} %bitcast.35), channel_id=1, source_target_pairs={{0,64},{16,464},{32,96},{48,496},{64,128},{80,16},{96,160},{112,48... | collective-permute-start | bytes 786440 | tf_op jit(solution)/shard_map/ppermute | solution.py:152
  22.7 0.0 collective-permute-done
  22.7 1.0 pad_maximum_fusion.rest_0_
  23.6 1.9 %collective-permute-start.1 = (bf16[256,1024]{1,0:T(8,128)(2,1)S(1)}, bf16[256,1024]{1,0:T(8,128)(2,1)S(1)}, u32[]{:S(2)}, u32[]{:S(2)}) collective-permute-start(bf16[256,1024]{1,0:T(8,128)(2,1)S(1)} %pad_maximum_fusion.rest_0_), channel_id=1, source_target_pairs={{0,32},{16,48},{32,0},{48,16},{64,96},{80,112},{96,64},{112,80},{1... | collective-permute-start | bytes 1572872 | tf_op jit(solution)/shard_map/ppermute | solution.py:152
  25.6 0.7 fusion.1
  26.3 0.0 collective-permute-done.5.rest_4_
  26.3 1.9 %collective-permute-start.6 = (bf16[128,1024]{1,0:T(8,128)(2,1)S(1)}, bf16[128,1024]{1,0:T(8,128)(2,1)}, u32[]{:S(2)}, u32[]{:S(2)}) collective-permute-start(bf16[128,1024]{1,0:T(8,128)(2,1)S(1)} %collective-permute-done.5.rest_4_), channel_id=1, source_target_pairs={{0,448},{16,80},{32,480},{48,112},{64,0},{80,144},{96,32},{112,176... | collective-permute-start | bytes 786440 | tf_op jit(solution)/shard_map/ppermute | solution.py:152
  28.2 0.0 copy-start.1
  28.2 0.7 copy-done.1
  28.9 0.0 collective-permute-done.2.rest_3_
  28.9 4.6 %collective-permute-start.3 = (bf16[128,1024]{1,0:T(8,128)(2,1)S(1)}, bf16[128,1024]{1,0:T(8,128)(2,1)}, u32[]{:S(2)}, u32[]{:S(2)}) collective-permute-start(bf16[128,1024]{1,0:T(8,128)(2,1)S(1)} %collective-permute-done.2.rest_3_), channel_id=1, source_target_pairs={{0,64},{16,464},{32,96},{48,496},{64,128},{80,16},{96,160},{112,48... | collective-permute-start | bytes 786440 | tf_op jit(solution)/shard_map/ppermute | solution.py:152
  33.5 0.0 copy-start.3
  33.5 0.7 copy-done.3
  35.5 0.1 stack.48.to_ref
  35.6 0.0 collective-permute-done.6.rest_6_
  35.6 1.9 %collective-permute-start.7 = (bf16[128,1024]{1,0:T(8,128)(2,1)}, bf16[128,1024]{1,0:T(8,128)(2,1)S(1)}, u32[]{:S(2)}, u32[]{:S(2)}) collective-permute-start(bf16[128,1024]{1,0:T(8,128)(2,1)} %collective-permute-done.6.rest_6_), channel_id=1, source_target_pairs={{0,448},{16,80},{32,480},{48,112},{64,0},{80,144},{96,32},{112,176... | collective-permute-start | bytes 786440 | tf_op jit(solution)/shard_map/ppermute | solution.py:152
  37.5 0.0 collective-permute-done.3.rest_5_
  37.6 4.6 %collective-permute-start.4 = (bf16[128,1024]{1,0:T(8,128)(2,1)}, bf16[128,1024]{1,0:T(8,128)(2,1)}, u32[]{:S(2)}, u32[]{:S(2)}) collective-permute-start(bf16[128,1024]{1,0:T(8,128)(2,1)} %collective-permute-done.3.rest_5_), channel_id=1, source_target_pairs={{0,64},{16,464},{32,96},{48,496},{64,128},{80,16},{96,160},{112,48... | collective-permute-start | bytes 786440 | tf_op jit(solution)/shard_map/ppermute | solution.py:152
  42.1 0.1 pad_maximum_fusion.1.scal_ref
  42.2 0.0 collective-permute-done.1.rest_1_
  42.2 0.0 copy-start
  42.2 0.9 copy-done
  43.2 0.0 copy-start.2
  43.2 0.9 copy-done.2
  44.1 0.0 copy-start.4
  44.1 0.9 copy-done.4
  45.1 6.2 %shard_map.92 = (f32[512,1024]{1,0:T(8,128)S(1)}, f32[3,128]{1,0:T(4,128)S(1)}, f32[1024,1024]{1,0:T(8,128)}) custom-call(s32[5]{0:T(128)S(1)} %add_multiply_fusion.1.base_ref, s32[5]{0:T(128)S(1)} %stack.48.to_ref, f32[2]{0:T(128)S(1)} %pad_maximum_fusion.1.scal_ref, s32[1,512]{1,0:T(1,128)S(1)} %bitcast.31, bf16[256,1024]{1,0:T(8,128)(2,1)S(1)} %pad_maximum_fusion.rest_0_, ...), custom_call_target="tpu_custom_call" | custom-call | flops 2013265920 | bytes 9175040 | tf_op jit(solution)/shard_map/pallas_call | solution.py:119
  51.3 0.0 collective-permute-done.7.rest_3_
  51.3 0.0 collective-permute-done.4.rest_2_
  51.3 1.9 %collective-permute-start.8 = (bf16[128,1024]{1,0:T(8,128)(2,1)}, bf16[128,1024]{1,0:T(8,128)(2,1)}, u32[]{:S(2)}, u32[]{:S(2)}) collective-permute-start(bf16[128,1024]{1,0:T(8,128)(2,1)} %collective-permute-done.4.rest_2_), channel_id=1, source_target_pairs={{0,64},{16,464},{32,96},{48,496},{64,128},{80,16},{96,160},{112,48... | collective-permute-start | bytes 786440 | tf_op jit(solution)/shard_map/ppermute | solution.py:152
  53.3 0.1 add_multiply_fusion
  53.4 3.3 %shard_map.93 = (f32[512,1024]{1,0:T(8,128)S(1)}, f32[3,128]{1,0:T(4,128)S(1)}, f32[1024,1024]{1,0:T(8,128)}) custom-call(s32[2]{0:T(128)S(1)} %get-tuple-element.37.base_ref, s32[2]{0:T(128)S(1)} %get-tuple-element.38.to_ref, f32[2]{0:T(128)S(1)} %pad_maximum_fusion.1.scal_ref, ...), custom_call_target="tpu_custom_call", output_to_operand_aliasing={{0}: (8, {}), {1}: (9, {}), {2}: (10, {})} | custom-call | flops 805306368 | bytes 6815744 | tf_op jit(solution)/shard_map/pallas_call | solution.py:119
  56.7 2.3 %collective-permute-done.8.rest_2_ = bf16[128,1024]{1,0:T(8,128)(2,1)} collective-permute-done((bf16[128,1024]{1,0:T(8,128)(2,1)}, bf16[128,1024]{1,0:T(8,128)(2,1)}, u32[]{:S(2)}, u32[]{:S(2)}) %collective-permute-start.8) | collective-permute-done | bytes 262176 | tf_op jit(solution)/shard_map/ppermute | solution.py:152
  59.0 2.8 %shard_map.94 = (f32[512,1024]{1,0:T(8,128)S(1)}, f32[3,128]{1,0:T(4,128)S(1)}, f32[1024,1024]{1,0:T(8,128)}) custom-call(s32[1]{0:T(128)S(6)} %mul.86.base_ref, s32[1]{0:T(128)} %bitcast.to_ref, f32[2]{0:T(128)S(1)} %pad_maximum_fusion.1.scal_ref, s32[1,512]{1,0:T(1,128)S(1)} %bitcast.33, ...), custom_call_target="tpu_custom_call", output_to_operand_aliasing={{0}: (7, {}), {1}: (8, {}), {2}: (9, {})} | custom-call | flops 402653184 | bytes 6029312 | tf_op jit(solution)/shard_map/pallas_call | solution.py:119
  61.8 0.0 reduce-scatter.2.cloned.1.call-update
  61.8 0.1 slice.22
  61.9 3.4 %collective-permute-start.9 = (f32[256,1024]{1,0:T(8,128)S(1)}, f32[256,1024]{1,0:T(8,128)}, u32[]{:S(2)}, u32[]{:S(2)}) collective-permute-start(f32[256,1024]{1,0:T(8,128)S(1)} %slice.22), channel_id=1, source_target_pairs={{0,32},{16,48},{32,0},{48,16},{64,96},{80,112},{96,64},{112,80},{1... | collective-permute-start | bytes 3145736 | tf_op jit(solution)/shard_map/ppermute | solution.py:152
  65.3 3.6 %psum.28 = f32[3,128]{1,0:T(4,128)S(1)} all-reduce(f32[3,128]{1,0:T(4,128)S(1)} %get-tuple-element.33), channel_id=1, replica_groups=mesh['y'=8,'x'=2,'c'=2,'z'=8,'h'=2] {'c'}, use_global_device_ids=true, to_apply=%region_0.1 | all-reduce | flops 384 | bytes 3072 | tf_op jit(solution)/shard_map/psum | solution.py:184
  68.9 19.5 %psum.29 = f32[3,128]{1,0:T(4,128)S(1)} all-reduce(f32[3,128]{1,0:T(4,128)S(1)} %psum.28), channel_id=1, replica_groups=mesh['y'=8,'x'=2,'c'=2,'z'=8,'h'=2] {'z'}, use_global_device_ids=true, to_apply=%region_1.2 | all-reduce | flops 384 | bytes 3072 | tf_op jit(solution)/shard_map/psum | solution.py:185
  88.4 9.5 %psum.30 = f32[3,128]{1,0:T(4,128)S(1)} all-reduce(f32[3,128]{1,0:T(4,128)S(1)} %psum.29), channel_id=1, replica_groups=mesh['y'=8,'x'=2,'c'=2,'z'=8,'h'=2] {'x','h'}, use_global_device_ids=true, to_apply=%region_2.3 | all-reduce | flops 384 | bytes 3072 | tf_op jit(solution)/shard_map/psum | solution.py:186
  97.9 0.0 collective-permute-done.9
  97.9 1.4 %slice_add_fusion = f32[256,1024]{1,0:T(8,128)S(1)} fusion(f32[256,1024]{1,0:T(8,128)} %collective-permute-done.9, f32[512,1024]{1,0:T(8,128)S(1)} %get-tuple-element.32), kind=kLoop, calls=%fused_computation | loop fusion | flops 262144 | bytes 3145728 | tf_op jit(solution)/shard_map/add | solution.py:188
  99.3 6.0 %collective-permute-start.10 = (f32[128,1024]{1,0:T(8,128)S(1)}, f32[128,1024]{1,0:T(8,128)S(1)}, u32[]{:S(2)}, u32[]{:S(2)}) collective-permute-start(f32[128,1024]{1,0:T(8,128)S(1)} %slice.29), channel_id=1, source_target_pairs={{0,16},{16,0},{32,48},{48,32},{64,80},{80,64},{96,112},{112,96},{1... | collective-permute-start | bytes 1572872 | tf_op jit(solution)/shard_map/ppermute | solution.py:152
  105.4 14.8 %psum.31 = f32[3,128]{1,0:T(4,128)S(1)} all-reduce(f32[3,128]{1,0:T(4,128)S(1)} %psum.30), channel_id=1, replica_groups=mesh['y'=8,'x'=2,'c'=2,'z'=8,'h'=2] {'y'}, use_global_device_ids=true, to_apply=%region_4.5 | all-reduce | flops 384 | bytes 3072 | tf_op jit(solution)/shard_map/psum | solution.py:190
  120.2 0.1 reduce_sum.9
  120.4 0.6 fusion.5
  121.0 0.0 collective-permute-done.10
  121.0 0.9 fusion
  121.8 0.0 reduce-scatter.2.cloned.1.call-done
  (4 shorter events, 0.1 us)
Async XLA Ops:
  7.2 114.7 %reduce-scatter.2.cloned.1.call-start = ((), (), s32[]{:S(2)}) async-start(), calls=%async_computation.1 | async-start | bytes 4718592 | tf_op jit(solution)/shard_map/reduce_scatter | solution.py:182
  7.2 15.4 %collective-permute-start = (bf16[128,1024]{1,0:T(8,128)(2,1)}, bf16[128,1024]{1,0:T(8,128)(2,1)S(1)}, u32[]{:S(2)}, u32[]{:S(2)}) collective-permute-start(bf16[128,1024]{1,0:T(8,128)(2,1)} %bitcast.37), channel_id=1, source_target_pairs={{0,16},{16,0},{32,48},{48,32},{64,80},{80,64},{96,112},{112,96},{1... | collective-permute-start | bytes 786440 | tf_op jit(solution)/shard_map/ppermute | solution.py:152
  16.0 10.3 %collective-permute-start.5 = (bf16[128,1024]{1,0:T(8,128)(2,1)}, bf16[128,1024]{1,0:T(8,128)(2,1)S(1)}, u32[]{:S(2)}, u32[]{:S(2)}) collective-permute-start(bf16[128,1024]{1,0:T(8,128)(2,1)} %bitcast.34), channel_id=1, source_target_pairs={{0,448},{16,80},{32,480},{48,112},{64,0},{80,144},{96,32},{112,176... | collective-permute-start | bytes 786440 | tf_op jit(solution)/shard_map/ppermute | solution.py:152
  17.9 11.0 %collective-permute-start.2 = (bf16[128,1024]{1,0:T(8,128)(2,1)}, bf16[128,1024]{1,0:T(8,128)(2,1)S(1)}, u32[]{:S(2)}, u32[]{:S(2)}) collective-permute-start(bf16[128,1024]{1,0:T(8,128)(2,1)} %bitcast.35), channel_id=1, source_target_pairs={{0,64},{16,464},{32,96},{48,496},{64,128},{80,16},{96,160},{112,48... | collective-permute-start | bytes 786440 | tf_op jit(solution)/shard_map/ppermute | solution.py:152
  23.6 18.6 %collective-permute-start.1 = (bf16[256,1024]{1,0:T(8,128)(2,1)S(1)}, bf16[256,1024]{1,0:T(8,128)(2,1)S(1)}, u32[]{:S(2)}, u32[]{:S(2)}) collective-permute-start(bf16[256,1024]{1,0:T(8,128)(2,1)S(1)} %pad_maximum_fusion.rest_0_), channel_id=1, source_target_pairs={{0,32},{16,48},{32,0},{48,16},{64,96},{80,112},{96,64},{112,80},{1... | collective-permute-start | bytes 1572872 | tf_op jit(solution)/shard_map/ppermute | solution.py:152
  26.3 9.3 %collective-permute-start.6 = (bf16[128,1024]{1,0:T(8,128)(2,1)S(1)}, bf16[128,1024]{1,0:T(8,128)(2,1)}, u32[]{:S(2)}, u32[]{:S(2)}) collective-permute-start(bf16[128,1024]{1,0:T(8,128)(2,1)S(1)} %collective-permute-done.5.rest_4_), channel_id=1, source_target_pairs={{0,448},{16,80},{32,480},{48,112},{64,0},{80,144},{96,32},{112,176... | collective-permute-start | bytes 786440 | tf_op jit(solution)/shard_map/ppermute | solution.py:152
  28.2 0.7 copy-start.1
  28.9 8.6 %collective-permute-start.3 = (bf16[128,1024]{1,0:T(8,128)(2,1)S(1)}, bf16[128,1024]{1,0:T(8,128)(2,1)}, u32[]{:S(2)}, u32[]{:S(2)}) collective-permute-start(bf16[128,1024]{1,0:T(8,128)(2,1)S(1)} %collective-permute-done.2.rest_3_), channel_id=1, source_target_pairs={{0,64},{16,464},{32,96},{48,496},{64,128},{80,16},{96,160},{112,48... | collective-permute-start | bytes 786440 | tf_op jit(solution)/shard_map/ppermute | solution.py:152
  33.5 0.7 copy-start.3
  35.6 15.7 %collective-permute-start.7 = (bf16[128,1024]{1,0:T(8,128)(2,1)}, bf16[128,1024]{1,0:T(8,128)(2,1)S(1)}, u32[]{:S(2)}, u32[]{:S(2)}) collective-permute-start(bf16[128,1024]{1,0:T(8,128)(2,1)} %collective-permute-done.6.rest_6_), channel_id=1, source_target_pairs={{0,448},{16,80},{32,480},{48,112},{64,0},{80,144},{96,32},{112,176... | collective-permute-start | bytes 786440 | tf_op jit(solution)/shard_map/ppermute | solution.py:152
  37.6 13.7 %collective-permute-start.4 = (bf16[128,1024]{1,0:T(8,128)(2,1)}, bf16[128,1024]{1,0:T(8,128)(2,1)}, u32[]{:S(2)}, u32[]{:S(2)}) collective-permute-start(bf16[128,1024]{1,0:T(8,128)(2,1)} %collective-permute-done.3.rest_5_), channel_id=1, source_target_pairs={{0,64},{16,464},{32,96},{48,496},{64,128},{80,16},{96,160},{112,48... | collective-permute-start | bytes 786440 | tf_op jit(solution)/shard_map/ppermute | solution.py:152
  42.2 1.0 copy-start
  43.2 0.9 copy-start.2
  44.1 0.9 copy-start.4
  51.3 7.7 %collective-permute-start.8 = (bf16[128,1024]{1,0:T(8,128)(2,1)}, bf16[128,1024]{1,0:T(8,128)(2,1)}, u32[]{:S(2)}, u32[]{:S(2)}) collective-permute-start(bf16[128,1024]{1,0:T(8,128)(2,1)} %collective-permute-done.4.rest_2_), channel_id=1, source_target_pairs={{0,64},{16,464},{32,96},{48,496},{64,128},{80,16},{96,160},{112,48... | collective-permute-start | bytes 786440 | tf_op jit(solution)/shard_map/ppermute | solution.py:152
  61.9 36.0 %collective-permute-start.9 = (f32[256,1024]{1,0:T(8,128)S(1)}, f32[256,1024]{1,0:T(8,128)}, u32[]{:S(2)}, u32[]{:S(2)}) collective-permute-start(f32[256,1024]{1,0:T(8,128)S(1)} %slice.22), channel_id=1, source_target_pairs={{0,32},{16,48},{32,0},{48,16},{64,96},{80,112},{96,64},{112,80},{1... | collective-permute-start | bytes 3145736 | tf_op jit(solution)/shard_map/ppermute | solution.py:152
  99.3 21.6 %collective-permute-start.10 = (f32[128,1024]{1,0:T(8,128)S(1)}, f32[128,1024]{1,0:T(8,128)S(1)}, u32[]{:S(2)}, u32[]{:S(2)}) collective-permute-start(f32[128,1024]{1,0:T(8,128)S(1)} %slice.29), channel_id=1, source_target_pairs={{0,16},{16,0},{32,48},{48,32},{64,80},{80,64},{96,112},{112,96},{1... | collective-permute-start | bytes 1572872 | tf_op jit(solution)/shard_map/ppermute | solution.py:152
Sparse Core Ops, SparseCore 0:
  62.0 59.0 reduce-scatter.1

commit v3 on v2

--- a/solution.py
+++ b/solution.py
@@ -173,10 +173,10 @@
         base = (to * (NX * NC) + x * NC + c) * rows
         return pairs(base.astype(jnp.int32), to, scal, idx, vs, rs, groups, carry)
 
-    carry = work((0, 1, -1, 2, -2), (r0, a1, b1, a2, b2), (1, 2, 2))
+    carry = work((1, -1, 2, -2), (a1, b1, a2, b2), (2, 2))
     a3, b3, *carry = tie(a3, b3, *carry)
     a4 = send(a3, with_a)
-    carry = work((3, -3), (a3, b3), (2,), carry)
+    carry = work((0, 3, -3), (r0, a3, b3), (1, 2), carry)
     ds, sums, do = work((4,), (a4,), (1,), carry)
 
     do = lax.psum_scatter(do, "y", scatter_dimension=0, tiled=True)

time: 129 us -> 127 us (0.984)
  waiting for transfers between devices: 2.34 us -> 0.27 us
    ppermute x11, waiting for transfers between devices: 2.32 us -> 0.25 us  [local(): send = lambda a, p: lax.ppermute(a, BLK, p)]
    unnamed x10 -> x14, local copies, waits for them, and re-layouts: 4.25 us -> 4.95 us
where the time goes in v3:
time: 127 us; the launch traced here: 126 us
  blocking collectives  46.7 us (37%)
  starting transfers between devices  41.5 us (33%)
  between operations  15.7 us (12%)
  Pallas kernels  12.1 us (10%)
  local copies, waits for them, and re-layouts  6.4 us (5%)
  other arithmetic  3.6 us (3%)
    ppermute x11, starting transfers between devices, local(): send = lambda a, p: lax.ppermute(a, BLK, p)  41.5 us
    psum x1, blocking collectives, local(): sums = lax.psum(sums, 'z')  19.8 us
    psum x1, blocking collectives, local(): sums = lax.psum(sums, 'y')  14.5 us
    pallas_call x3, Pallas kernels, pairs(): pl.pallas_call(functools.partial(pair_kernel, 1.0 / math.sqrt(d), not car...  12.1 us
    psum x1, blocking collectives, local(): sums = lax.psum(sums, ('x', 'h'))  8.91 us
    unnamed x14, local copies, waits for them, and re-layouts  4.95 us
    psum x1, blocking collectives, local(): sums = lax.psum(sums, 'c')  3.52 us
  transfers between devices with their start and end apart: 12, of which 1 were waited for; matrix products, arithmetic and copies ran while one was open for 4% of the time, Pallas kernels for 7%

profile of v3, /device:TPU:1, one launch (start us, length us, event | category | flops | bytes accessed | tf_op | source)
XLA Modules:
  0.0 126.4 jit_solution(2171275391997617518)
XLA Ops:
  7.2 0.0 reduce-scatter.2.cloned.1.call-start
  7.2 8.8 %collective-permute-start = (bf16[128,1024]{1,0:T(8,128)(2,1)}, bf16[128,1024]{1,0:T(8,128)(2,1)S(1)}, u32[]{:S(2)}, u32[]{:S(2)}) collective-permute-start(bf16[128,1024]{1,0:T(8,128)(2,1)} %bitcast.37), channel_id=1, source_target_pairs={{0,16},{16,0},{32,48},{48,32},{64,80},{80,64},{96,112},{112,96},{1... | collective-permute-start | bytes 786440 | tf_op jit(solution)/shard_map/ppermute | solution.py:152
  16.0 1.9 %collective-permute-start.5 = (bf16[128,1024]{1,0:T(8,128)(2,1)}, bf16[128,1024]{1,0:T(8,128)(2,1)S(1)}, u32[]{:S(2)}, u32[]{:S(2)}) collective-permute-start(bf16[128,1024]{1,0:T(8,128)(2,1)} %bitcast.31), channel_id=1, source_target_pairs={{0,448},{16,80},{32,480},{48,112},{64,0},{80,144},{96,32},{112,176... | collective-permute-start | bytes 786440 | tf_op jit(solution)/shard_map/ppermute | solution.py:152
  17.9 4.6 %collective-permute-start.2 = (bf16[128,1024]{1,0:T(8,128)(2,1)}, bf16[128,1024]{1,0:T(8,128)(2,1)S(1)}, u32[]{:S(2)}, u32[]{:S(2)}) collective-permute-start(bf16[128,1024]{1,0:T(8,128)(2,1)} %bitcast.32), channel_id=1, source_target_pairs={{0,64},{16,464},{32,96},{48,496},{64,128},{80,16},{96,160},{112,48... | collective-permute-start | bytes 786440 | tf_op jit(solution)/shard_map/ppermute | solution.py:152
  22.5 0.0 collective-permute-done
  22.5 1.0 pad_maximum_fusion.rest_0_
  23.5 1.9 %collective-permute-start.1 = (bf16[256,1024]{1,0:T(8,128)(2,1)S(1)}, bf16[256,1024]{1,0:T(8,128)(2,1)S(1)}, u32[]{:S(2)}, u32[]{:S(2)}) collective-permute-start(bf16[256,1024]{1,0:T(8,128)(2,1)S(1)} %pad_maximum_fusion.rest_0_), channel_id=1, source_target_pairs={{0,32},{16,48},{32,0},{48,16},{64,96},{80,112},{96,64},{112,80},{1... | collective-permute-start | bytes 1572872 | tf_op jit(solution)/shard_map/ppermute | solution.py:152
  25.6 0.0 collective-permute-done.5.rest_3_
  25.6 1.9 %collective-permute-start.6 = (bf16[128,1024]{1,0:T(8,128)(2,1)S(1)}, bf16[128,1024]{1,0:T(8,128)(2,1)}, u32[]{:S(2)}, u32[]{:S(2)}) collective-permute-start(bf16[128,1024]{1,0:T(8,128)(2,1)S(1)} %collective-permute-done.5.rest_3_), channel_id=1, source_target_pairs={{0,448},{16,80},{32,480},{48,112},{64,0},{80,144},{96,32},{112,176... | collective-permute-start | bytes 786440 | tf_op jit(solution)/shard_map/ppermute | solution.py:152
  27.5 0.0 copy-start.3
  27.5 0.7 copy-done.3
  28.2 0.0 collective-permute-done.2.rest_2_
  28.2 4.6 %collective-permute-start.3 = (bf16[128,1024]{1,0:T(8,128)(2,1)S(1)}, bf16[128,1024]{1,0:T(8,128)(2,1)}, u32[]{:S(2)}, u32[]{:S(2)}) collective-permute-start(bf16[128,1024]{1,0:T(8,128)(2,1)S(1)} %collective-permute-done.2.rest_2_), channel_id=1, source_target_pairs={{0,64},{16,464},{32,96},{48,496},{64,128},{80,16},{96,160},{112,48... | collective-permute-start | bytes 786440 | tf_op jit(solution)/shard_map/ppermute | solution.py:152
  32.8 0.0 copy-start.5
  32.8 0.7 copy-done.5
  33.5 0.1 add_multiply_fusion.1
  34.9 0.7 fusion.1
  35.6 0.0 collective-permute-done.6.rest_5_
  35.6 1.9 %collective-permute-start.7 = (bf16[128,1024]{1,0:T(8,128)(2,1)}, bf16[128,1024]{1,0:T(8,128)(2,1)S(1)}, u32[]{:S(2)}, u32[]{:S(2)}) collective-permute-start(bf16[128,1024]{1,0:T(8,128)(2,1)} %collective-permute-done.6.rest_5_), channel_id=1, source_target_pairs={{0,448},{16,80},{32,480},{48,112},{64,0},{80,144},{96,32},{112,176... | collective-permute-start | bytes 786440 | tf_op jit(solution)/shard_map/ppermute | solution.py:152
  37.6 0.0 collective-permute-done.3.rest_4_
  37.6 4.6 %collective-permute-start.4 = (bf16[128,1024]{1,0:T(8,128)(2,1)}, bf16[128,1024]{1,0:T(8,128)(2,1)}, u32[]{:S(2)}, u32[]{:S(2)}) collective-permute-start(bf16[128,1024]{1,0:T(8,128)(2,1)} %collective-permute-done.3.rest_4_), channel_id=1, source_target_pairs={{0,64},{16,464},{32,96},{48,496},{64,128},{80,16},{96,160},{112,48... | collective-permute-start | bytes 786440 | tf_op jit(solution)/shard_map/ppermute | solution.py:152
  42.1 0.1 pad_maximum_fusion.1.scal_ref
  42.2 0.0 collective-permute-done.1.rest_1_
  42.2 0.0 copy-start.4
  42.2 0.9 copy-done.4
  43.2 0.0 copy-start.6
  43.2 0.9 copy-done.6
  44.1 0.0 copy-start
  44.1 4.9 %shard_map.92 = (f32[512,1024]{1,0:T(8,128)S(1)}, f32[3,128]{1,0:T(4,128)S(1)}, f32[1024,1024]{1,0:T(8,128)}) custom-call(s32[4]{0:T(128)S(1)} %get-tuple-element.39.base_ref, s32[4]{0:T(128)S(1)} %get-tuple-element.40.to_ref, f32[2]{0:T(128)S(1)} %pad_maximum_fusion.1.scal_ref, s32[1,512]{1,0:T(1,128)S(1)} %bitcast.34, ...), custom_call_target="tpu_custom_call" | custom-call | flops 1610612736 | bytes 8388608 | tf_op jit(solution)/shard_map/pallas_call | solution.py:119
  49.0 0.0 collective-permute-done.7.rest_4_
  49.0 0.0 copy-start.1
  49.0 0.7 copy-done.1
  49.7 0.0 collective-permute-done.4.rest_3_
  49.7 1.9 %collective-permute-start.8 = (bf16[128,1024]{1,0:T(8,128)(2,1)}, bf16[128,1024]{1,0:T(8,128)(2,1)}, u32[]{:S(2)}, u32[]{:S(2)}) collective-permute-start(bf16[128,1024]{1,0:T(8,128)(2,1)} %collective-permute-done.4.rest_3_), channel_id=1, source_target_pairs={{0,64},{16,464},{32,96},{48,496},{64,128},{80,16},{96,160},{112,48... | collective-permute-start | bytes 786440 | tf_op jit(solution)/shard_map/ppermute | solution.py:152
  51.7 0.1 add_multiply_fusion
  51.8 0.0 copy-done
  51.8 0.0 copy-start.2
  51.8 1.0 copy-done.2
  52.8 4.4 %shard_map.93 = (f32[512,1024]{1,0:T(8,128)S(1)}, f32[3,128]{1,0:T(4,128)S(1)}, f32[1024,1024]{1,0:T(8,128)}) custom-call(s32[3]{0:T(128)S(1)} %get-tuple-element.37.base_ref, s32[3]{0:T(128)S(1)} %get-tuple-element.38.to_ref, f32[2]{0:T(128)S(1)} %pad_maximum_fusion.1.scal_ref, ...), custom_call_target="tpu_custom_call", output_to_operand_aliasing={{0}: (9, {}), {1}: (10, {}), {2}: (11, {})} | custom-call | flops 1207959552 | bytes 7602176 | tf_op jit(solution)/shard_map/pallas_call | solution.py:119
  57.2 0.2 collective-permute-done.8.rest_2_
  57.4 2.8 %shard_map.94 = (f32[512,1024]{1,0:T(8,128)S(1)}, f32[3,128]{1,0:T(4,128)S(1)}, f32[1024,1024]{1,0:T(8,128)}) custom-call(s32[1]{0:T(128)S(6)} %mul.86.base_ref, s32[1]{0:T(128)} %bitcast.to_ref, f32[2]{0:T(128)S(1)} %pad_maximum_fusion.1.scal_ref, s32[1,512]{1,0:T(1,128)S(1)} %bitcast.36, ...), custom_call_target="tpu_custom_call", output_to_operand_aliasing={{0}: (7, {}), {1}: (8, {}), {2}: (9, {})} | custom-call | flops 402653184 | bytes 6029312 | tf_op jit(solution)/shard_map/pallas_call | solution.py:119
  60.2 0.0 reduce-scatter.2.cloned.1.call-update
  60.3 0.1 slice.22
  60.4 3.4 %collective-permute-start.9 = (f32[256,1024]{1,0:T(8,128)S(1)}, f32[256,1024]{1,0:T(8,128)}, u32[]{:S(2)}, u32[]{:S(2)}) collective-permute-start(f32[256,1024]{1,0:T(8,128)S(1)} %slice.22), channel_id=1, source_target_pairs={{0,32},{16,48},{32,0},{48,16},{64,96},{80,112},{96,64},{112,80},{1... | collective-permute-start | bytes 3145736 | tf_op jit(solution)/shard_map/ppermute | solution.py:152
  63.7 3.5 %psum.28 = f32[3,128]{1,0:T(4,128)S(1)} all-reduce(f32[3,128]{1,0:T(4,128)S(1)} %get-tuple-element.33), channel_id=1, replica_groups=mesh['y'=8,'x'=2,'c'=2,'z'=8,'h'=2] {'c'}, use_global_device_ids=true, to_apply=%region_0.1 | all-reduce | flops 384 | bytes 3072 | tf_op jit(solution)/shard_map/psum | solution.py:184
  67.3 19.8 %psum.29 = f32[3,128]{1,0:T(4,128)S(1)} all-reduce(f32[3,128]{1,0:T(4,128)S(1)} %psum.28), channel_id=1, replica_groups=mesh['y'=8,'x'=2,'c'=2,'z'=8,'h'=2] {'z'}, use_global_device_ids=true, to_apply=%region_1.2 | all-reduce | flops 384 | bytes 3072 | tf_op jit(solution)/shard_map/psum | solution.py:185
  87.0 8.9 %psum.30 = f32[3,128]{1,0:T(4,128)S(1)} all-reduce(f32[3,128]{1,0:T(4,128)S(1)} %psum.29), channel_id=1, replica_groups=mesh['y'=8,'x'=2,'c'=2,'z'=8,'h'=2] {'x','h'}, use_global_device_ids=true, to_apply=%region_2.3 | all-reduce | flops 384 | bytes 3072 | tf_op jit(solution)/shard_map/psum | solution.py:186
  96.0 0.0 collective-permute-done.9
  96.0 1.4 %slice_add_fusion = f32[256,1024]{1,0:T(8,128)S(1)} fusion(f32[256,1024]{1,0:T(8,128)} %collective-permute-done.9, f32[512,1024]{1,0:T(8,128)S(1)} %get-tuple-element.32), kind=kLoop, calls=%fused_computation | loop fusion | flops 262144 | bytes 3145728 | tf_op jit(solution)/shard_map/add | solution.py:188
  97.4 6.0 %collective-permute-start.10 = (f32[128,1024]{1,0:T(8,128)S(1)}, f32[128,1024]{1,0:T(8,128)S(1)}, u32[]{:S(2)}, u32[]{:S(2)}) collective-permute-start(f32[128,1024]{1,0:T(8,128)S(1)} %slice.29), channel_id=1, source_target_pairs={{0,16},{16,0},{32,48},{48,32},{64,80},{80,64},{96,112},{112,96},{1... | collective-permute-start | bytes 1572872 | tf_op jit(solution)/shard_map/ppermute | solution.py:152
  103.4 14.5 %psum.31 = f32[3,128]{1,0:T(4,128)S(1)} all-reduce(f32[3,128]{1,0:T(4,128)S(1)} %psum.30), channel_id=1, replica_groups=mesh['y'=8,'x'=2,'c'=2,'z'=8,'h'=2] {'y'}, use_global_device_ids=true, to_apply=%region_4.5 | all-reduce | flops 384 | bytes 3072 | tf_op jit(solution)/shard_map/psum | solution.py:190
  118.0 0.1 reduce_sum.9
  118.1 0.6 fusion.5
  118.7 0.0 collective-permute-done.10
  118.7 0.9 fusion
  119.5 0.0 reduce-scatter.2.cloned.1.call-done
  (3 shorter events, 0.1 us)
Async XLA Ops:
  7.2 112.4 %reduce-scatter.2.cloned.1.call-start = ((), (), s32[]{:S(2)}) async-start(), calls=%async_computation.1 | async-start | bytes 4718592 | tf_op jit(solution)/shard_map/reduce_scatter | solution.py:182
  7.2 15.3 %collective-permute-start = (bf16[128,1024]{1,0:T(8,128)(2,1)}, bf16[128,1024]{1,0:T(8,128)(2,1)S(1)}, u32[]{:S(2)}, u32[]{:S(2)}) collective-permute-start(bf16[128,1024]{1,0:T(8,128)(2,1)} %bitcast.37), channel_id=1, source_target_pairs={{0,16},{16,0},{32,48},{48,32},{64,80},{80,64},{96,112},{112,96},{1... | collective-permute-start | bytes 786440 | tf_op jit(solution)/shard_map/ppermute | solution.py:152
  16.0 9.6 %collective-permute-start.5 = (bf16[128,1024]{1,0:T(8,128)(2,1)}, bf16[128,1024]{1,0:T(8,128)(2,1)S(1)}, u32[]{:S(2)}, u32[]{:S(2)}) collective-permute-start(bf16[128,1024]{1,0:T(8,128)(2,1)} %bitcast.31), channel_id=1, source_target_pairs={{0,448},{16,80},{32,480},{48,112},{64,0},{80,144},{96,32},{112,176... | collective-permute-start | bytes 786440 | tf_op jit(solution)/shard_map/ppermute | solution.py:152
  17.9 10.3 %collective-permute-start.2 = (bf16[128,1024]{1,0:T(8,128)(2,1)}, bf16[128,1024]{1,0:T(8,128)(2,1)S(1)}, u32[]{:S(2)}, u32[]{:S(2)}) collective-permute-start(bf16[128,1024]{1,0:T(8,128)(2,1)} %bitcast.32), channel_id=1, source_target_pairs={{0,64},{16,464},{32,96},{48,496},{64,128},{80,16},{96,160},{112,48... | collective-permute-start | bytes 786440 | tf_op jit(solution)/shard_map/ppermute | solution.py:152
  23.5 18.7 %collective-permute-start.1 = (bf16[256,1024]{1,0:T(8,128)(2,1)S(1)}, bf16[256,1024]{1,0:T(8,128)(2,1)S(1)}, u32[]{:S(2)}, u32[]{:S(2)}) collective-permute-start(bf16[256,1024]{1,0:T(8,128)(2,1)S(1)} %pad_maximum_fusion.rest_0_), channel_id=1, source_target_pairs={{0,32},{16,48},{32,0},{48,16},{64,96},{80,112},{96,64},{112,80},{1... | collective-permute-start | bytes 1572872 | tf_op jit(solution)/shard_map/ppermute | solution.py:152
  25.6 10.0 %collective-permute-start.6 = (bf16[128,1024]{1,0:T(8,128)(2,1)S(1)}, bf16[128,1024]{1,0:T(8,128)(2,1)}, u32[]{:S(2)}, u32[]{:S(2)}) collective-permute-start(bf16[128,1024]{1,0:T(8,128)(2,1)S(1)} %collective-permute-done.5.rest_3_), channel_id=1, source_target_pairs={{0,448},{16,80},{32,480},{48,112},{64,0},{80,144},{96,32},{112,176... | collective-permute-start | bytes 786440 | tf_op jit(solution)/shard_map/ppermute | solution.py:152
  27.5 0.7 copy-start.3
  28.2 9.3 %collective-permute-start.3 = (bf16[128,1024]{1,0:T(8,128)(2,1)S(1)}, bf16[128,1024]{1,0:T(8,128)(2,1)}, u32[]{:S(2)}, u32[]{:S(2)}) collective-permute-start(bf16[128,1024]{1,0:T(8,128)(2,1)S(1)} %collective-permute-done.2.rest_2_), channel_id=1, source_target_pairs={{0,64},{16,464},{32,96},{48,496},{64,128},{80,16},{96,160},{112,48... | collective-permute-start | bytes 786440 | tf_op jit(solution)/shard_map/ppermute | solution.py:152
  32.8 0.7 copy-start.5
  35.6 13.4 %collective-permute-start.7 = (bf16[128,1024]{1,0:T(8,128)(2,1)}, bf16[128,1024]{1,0:T(8,128)(2,1)S(1)}, u32[]{:S(2)}, u32[]{:S(2)}) collective-permute-start(bf16[128,1024]{1,0:T(8,128)(2,1)} %collective-permute-done.6.rest_5_), channel_id=1, source_target_pairs={{0,448},{16,80},{32,480},{48,112},{64,0},{80,144},{96,32},{112,176... | collective-permute-start | bytes 786440 | tf_op jit(solution)/shard_map/ppermute | solution.py:152
  37.6 12.2 %collective-permute-start.4 = (bf16[128,1024]{1,0:T(8,128)(2,1)}, bf16[128,1024]{1,0:T(8,128)(2,1)}, u32[]{:S(2)}, u32[]{:S(2)}) collective-permute-start(bf16[128,1024]{1,0:T(8,128)(2,1)} %collective-permute-done.3.rest_4_), channel_id=1, source_target_pairs={{0,64},{16,464},{32,96},{48,496},{64,128},{80,16},{96,160},{112,48... | collective-permute-start | bytes 786440 | tf_op jit(solution)/shard_map/ppermute | solution.py:152
  42.2 1.0 copy-start.4
  43.2 0.9 copy-start.6
  44.1 7.7 %copy-start = (bf16[1,128,1024]{2,1,0:T(8,128)(2,1)S(1)}, bf16[1,128,1024]{2,1,0:T(8,128)(2,1)}, u32[]{:S(2)}) copy-start(bf16[1,128,1024]{2,1,0:T(8,128)(2,1)} %param.6) | copy-start | bytes 786436
  49.0 0.7 copy-start.1
  49.7 7.7 %collective-permute-start.8 = (bf16[128,1024]{1,0:T(8,128)(2,1)}, bf16[128,1024]{1,0:T(8,128)(2,1)}, u32[]{:S(2)}, u32[]{:S(2)}) collective-permute-start(bf16[128,1024]{1,0:T(8,128)(2,1)} %collective-permute-done.4.rest_3_), channel_id=1, source_target_pairs={{0,64},{16,464},{32,96},{48,496},{64,128},{80,16},{96,160},{112,48... | collective-permute-start | bytes 786440 | tf_op jit(solution)/shard_map/ppermute | solution.py:152
  51.8 1.0 copy-start.2
  60.4 35.6 %collective-permute-start.9 = (f32[256,1024]{1,0:T(8,128)S(1)}, f32[256,1024]{1,0:T(8,128)}, u32[]{:S(2)}, u32[]{:S(2)}) collective-permute-start(f32[256,1024]{1,0:T(8,128)S(1)} %slice.22), channel_id=1, source_target_pairs={{0,32},{16,48},{32,0},{48,16},{64,96},{80,112},{96,64},{112,80},{1... | collective-permute-start | bytes 3145736 | tf_op jit(solution)/shard_map/ppermute | solution.py:152
  97.4 21.3 %collective-permute-start.10 = (f32[128,1024]{1,0:T(8,128)S(1)}, f32[128,1024]{1,0:T(8,128)S(1)}, u32[]{:S(2)}, u32[]{:S(2)}) collective-permute-start(f32[128,1024]{1,0:T(8,128)S(1)} %slice.29), channel_id=1, source_target_pairs={{0,16},{16,0},{32,48},{48,32},{64,80},{80,64},{96,112},{112,96},{1... | collective-permute-start | bytes 1572872 | tf_op jit(solution)/shard_map/ppermute | solution.py:152
Sparse Core Ops, SparseCore 0:
  60.4 58.9 reduce-scatter.1

commit v4 on v3

--- a/solution.py
+++ b/solution.py
@@ -174,8 +174,7 @@
         return pairs(base.astype(jnp.int32), to, scal, idx, vs, rs, groups, carry)
 
     carry = work((1, -1, 2, -2), (a1, b1, a2, b2), (2, 2))
-    a3, b3, *carry = tie(a3, b3, *carry)
-    a4 = send(a3, with_a)
+    a4 = send(b3, with_b)
     carry = work((0, 3, -3), (r0, a3, b3), (1, 2), carry)
     ds, sums, do = work((4,), (a4,), (1,), carry)
 

time: 127 us -> 127 us (level)
  waiting for transfers between devices: 0.27 us -> 2.54 us
  starting transfers between devices: 41.5 us -> 39.5 us
    psum x1, blocking collectives: 3.52 us -> 7.49 us  [local(): sums = lax.psum(sums, 'c')]
    psum x1, blocking collectives: 19.8 us -> 17.6 us  [local(): sums = lax.psum(sums, 'z')]
    ppermute x11, starting transfers between devices: 41.5 us -> 39.5 us  [local(): send = lambda a, p: lax.ppermute(a, BLK, p)]
    reduce_scatter x1, waiting for transfers between devices: 0.01 us -> 1.64 us  [local(): do = lax.psum_scatter(do, 'y', scatter_dimension=0, tiled=True)]
    psum x1, blocking collectives: 14.5 us -> 13.1 us  [local(): sums = lax.psum(sums, 'y')]
  transfers between devices with their start and end apart: 12 -> 12, of which waited for: 1 -> 2; matrix products, arithmetic and copies ran while one was open for 4% -> 4% of each run, Pallas kernels for 7% -> 7%
where the time goes in v4:
time: 127 us; the launch traced here: 126 us
  blocking collectives  47.7 us (38%)
  starting transfers between devices  39.5 us (31%)
  between operations  15.8 us (12%)
  Pallas kernels  11.2 us (9%)
  local copies, waits for them, and re-layouts  5.71 us (4%)
  other arithmetic  3.58 us (3%)
  waiting for transfers between devices  2.54 us (2%)
    ppermute x11, starting transfers between devices, local(): send = lambda a, p: lax.ppermute(a, BLK, p)  39.5 us
    psum x1, blocking collectives, local(): sums = lax.psum(sums, 'z')  17.6 us
    psum x1, blocking collectives, local(): sums = lax.psum(sums, 'y')  13.1 us
    pallas_call x3, Pallas kernels, pairs(): pl.pallas_call(functools.partial(pair_kernel, 1.0 / math.sqrt(d), not car...  11.2 us
    psum x1, blocking collectives, local(): sums = lax.psum(sums, ('x', 'h'))  9.55 us
    psum x1, blocking collectives, local(): sums = lax.psum(sums, 'c')  7.49 us
    unnamed x14, local copies, waits for them, and re-layouts  4.26 us
  transfers between devices with their start and end apart: 12, of which 2 were waited for; matrix products, arithmetic and copies ran while one was open for 4% of the time, Pallas kernels for 7%

profile of v4, /device:TPU:1, one launch (start us, length us, event | category | flops | bytes accessed | tf_op | source)
XLA Modules:
  0.0 126.0 jit_solution(12427218062501308522)
XLA Ops:
  7.2 0.0 reduce-scatter.2.cloned.1.call-start
  7.2 4.0 %collective-permute-start.2 = (bf16[128,1024]{1,0:T(8,128)(2,1)}, bf16[128,1024]{1,0:T(8,128)(2,1)S(1)}, u32[]{:S(2)}, u32[]{:S(2)}) collective-permute-start(bf16[128,1024]{1,0:T(8,128)(2,1)} %bitcast.31), channel_id=1, source_target_pairs={{0,448},{16,80},{32,480},{48,112},{64,0},{80,144},{96,32},{112,176... | collective-permute-start | bytes 786440 | tf_op jit(solution)/shard_map/ppermute | solution.py:152
  11.3 6.7 %collective-permute-start = (bf16[128,1024]{1,0:T(8,128)(2,1)}, bf16[128,1024]{1,0:T(8,128)(2,1)S(1)}, u32[]{:S(2)}, u32[]{:S(2)}) collective-permute-start(bf16[128,1024]{1,0:T(8,128)(2,1)} %bitcast.37), channel_id=1, source_target_pairs={{0,16},{16,0},{32,48},{48,32},{64,80},{80,64},{96,112},{112,96},{1... | collective-permute-start | bytes 786440 | tf_op jit(solution)/shard_map/ppermute | solution.py:152
  17.9 1.9 %collective-permute-start.6 = (bf16[128,1024]{1,0:T(8,128)(2,1)}, bf16[128,1024]{1,0:T(8,128)(2,1)S(1)}, u32[]{:S(2)}, u32[]{:S(2)}) collective-permute-start(bf16[128,1024]{1,0:T(8,128)(2,1)} %bitcast.32), channel_id=1, source_target_pairs={{0,64},{16,464},{32,96},{48,496},{64,128},{80,16},{96,160},{112,48... | collective-permute-start | bytes 786440 | tf_op jit(solution)/shard_map/ppermute | solution.py:152
  20.0 0.0 collective-permute-done.2.rest_3_
  20.0 0.0 copy-start.1
  20.1 3.6 %collective-permute-start.3 = (bf16[128,1024]{1,0:T(8,128)(2,1)S(1)}, bf16[128,1024]{1,0:T(8,128)(2,1)S(1)}, u32[]{:S(2)}, u32[]{:S(2)}) collective-permute-start(bf16[128,1024]{1,0:T(8,128)(2,1)S(1)} %collective-permute-done.2.rest_3_), channel_id=1, source_target_pairs={{0,448},{16,80},{32,480},{48,112},{64,0},{80,144},{96,32},{112,176... | collective-permute-start | bytes 786440 | tf_op jit(solution)/shard_map/ppermute | solution.py:152
  23.7 0.0 collective-permute-done
  23.7 1.0 pad_maximum_fusion.rest_0_
  24.7 1.9 %collective-permute-start.1 = (bf16[256,1024]{1,0:T(8,128)(2,1)S(1)}, bf16[256,1024]{1,0:T(8,128)(2,1)S(1)}, u32[]{:S(2)}, u32[]{:S(2)}) collective-permute-start(bf16[256,1024]{1,0:T(8,128)(2,1)S(1)} %pad_maximum_fusion.rest_0_), channel_id=1, source_target_pairs={{0,32},{16,48},{32,0},{48,16},{64,96},{80,112},{96,64},{112,80},{1... | collective-permute-start | bytes 1572872 | tf_op jit(solution)/shard_map/ppermute | solution.py:152
  26.6 0.7 fusion.1
  27.4 0.0 collective-permute-done.6.rest_2_
  27.4 3.2 %collective-permute-start.7 = (bf16[128,1024]{1,0:T(8,128)(2,1)S(1)}, bf16[128,1024]{1,0:T(8,128)(2,1)}, u32[]{:S(2)}, u32[]{:S(2)}) collective-permute-start(bf16[128,1024]{1,0:T(8,128)(2,1)S(1)} %collective-permute-done.6.rest_2_), channel_id=1, source_target_pairs={{0,64},{16,464},{32,96},{48,496},{64,128},{80,16},{96,160},{112,48... | collective-permute-start | bytes 786440 | tf_op jit(solution)/shard_map/ppermute | solution.py:152
  30.5 0.0 copy-start.3
  30.6 0.7 copy-done.3
  31.2 0.1 add_multiply_fusion.1
  31.3 0.0 copy-done.1
  31.3 0.0 collective-permute-done.3.rest_5_
  31.4 2.1 %collective-permute-start.4 = (bf16[128,1024]{1,0:T(8,128)(2,1)S(1)}, bf16[128,1024]{1,0:T(8,128)(2,1)S(1)}, u32[]{:S(2)}, u32[]{:S(2)}) collective-permute-start(bf16[128,1024]{1,0:T(8,128)(2,1)S(1)} %collective-permute-done.3.rest_5_), channel_id=1, source_target_pairs={{0,448},{16,80},{32,480},{48,112},{64,0},{80,144},{96,32},{112,176... | collective-permute-start | bytes 786440 | tf_op jit(solution)/shard_map/ppermute | solution.py:152
  33.5 0.0 copy-start.5
  33.5 0.7 copy-done.5
  34.2 0.1 add_multiply_fusion
  35.6 0.0 collective-permute-done.7.rest_4_
  35.6 4.4 %collective-permute-start.8 = (bf16[128,1024]{1,0:T(8,128)(2,1)}, bf16[128,1024]{1,0:T(8,128)(2,1)S(1)}, u32[]{:S(2)}, u32[]{:S(2)}) collective-permute-start(bf16[128,1024]{1,0:T(8,128)(2,1)} %collective-permute-done.7.rest_4_), channel_id=1, source_target_pairs={{0,64},{16,464},{32,96},{48,496},{64,128},{80,16},{96,160},{112,48... | collective-permute-start | bytes 786440 | tf_op jit(solution)/shard_map/ppermute | solution.py:152
  40.0 0.1 pad_maximum_fusion.1.scal_ref
  40.1 0.9 collective-permute-done.4.rest_4_
  40.9 1.9 %collective-permute-start.5 = (bf16[128,1024]{1,0:T(8,128)(2,1)S(1)}, bf16[128,1024]{1,0:T(8,128)(2,1)S(1)}, u32[]{:S(2)}, u32[]{:S(2)}) collective-permute-start(bf16[128,1024]{1,0:T(8,128)(2,1)S(1)} %collective-permute-done.4.rest_4_), channel_id=1, source_target_pairs={{0,448},{16,80},{32,480},{48,112},{64,0},{80,144},{96,32},{112,176... | collective-permute-start | bytes 786440 | tf_op jit(solution)/shard_map/ppermute | solution.py:152
  42.8 0.0 collective-permute-done.1.rest_1_
  42.9 0.0 copy-start.2
  42.9 0.9 copy-done.2
  43.8 0.0 copy-start.4
  43.8 0.9 copy-done.4
  44.8 0.0 copy-start.6
  44.8 0.9 copy-done.6
  45.7 0.0 copy-start
  45.7 4.8 %shard_map.92 = (f32[512,1024]{1,0:T(8,128)S(1)}, f32[3,128]{1,0:T(4,128)S(1)}, f32[1024,1024]{1,0:T(8,128)}) custom-call(s32[4]{0:T(128)S(1)} %get-tuple-element.27.base_ref, s32[4]{0:T(128)S(1)} %get-tuple-element.28.to_ref, f32[2]{0:T(128)S(1)} %pad_maximum_fusion.1.scal_ref, s32[1,512]{1,0:T(1,128)S(1)} %bitcast.34, ...), custom_call_target="tpu_custom_call" | custom-call | flops 1610612736 | bytes 8388608 | tf_op jit(solution)/shard_map/pallas_call | solution.py:119
  50.5 0.0 collective-permute-done.8.rest_3_
  50.5 0.0 copy-done
  50.6 4.0 %shard_map.93 = (f32[512,1024]{1,0:T(8,128)S(1)}, f32[3,128]{1,0:T(4,128)S(1)}, f32[1024,1024]{1,0:T(8,128)}) custom-call(s32[3]{0:T(128)S(1)} %get-tuple-element.29.base_ref, s32[3]{0:T(128)S(1)} %get-tuple-element.30.to_ref, f32[2]{0:T(128)S(1)} %pad_maximum_fusion.1.scal_ref, ...), custom_call_target="tpu_custom_call", output_to_operand_aliasing={{0}: (9, {}), {1}: (10, {}), {2}: (11, {})} | custom-call | flops 1207959552 | bytes 7602176 | tf_op jit(solution)/shard_map/pallas_call | solution.py:119
  54.6 0.0 collective-permute-done.5.rest_2_
  54.6 2.4 %shard_map.94 = (f32[512,1024]{1,0:T(8,128)S(1)}, f32[3,128]{1,0:T(4,128)S(1)}, f32[1024,1024]{1,0:T(8,128)}) custom-call(s32[1]{0:T(128)S(6)} %mul.86.base_ref, s32[1]{0:T(128)} %bitcast.to_ref, f32[2]{0:T(128)S(1)} %pad_maximum_fusion.1.scal_ref, s32[1,512]{1,0:T(1,128)S(1)} %bitcast.36, ...), custom_call_target="tpu_custom_call", output_to_operand_aliasing={{0}: (7, {}), {1}: (8, {}), {2}: (9, {})} | custom-call | flops 402653184 | bytes 6029312 | tf_op jit(solution)/shard_map/pallas_call | solution.py:119
  57.0 0.0 reduce-scatter.2.cloned.1.call-update
  57.0 0.1 slice.22
  57.1 3.6 %collective-permute-start.9 = (f32[256,1024]{1,0:T(8,128)S(1)}, f32[256,1024]{1,0:T(8,128)}, u32[]{:S(2)}, u32[]{:S(2)}) collective-permute-start(f32[256,1024]{1,0:T(8,128)S(1)} %slice.22), channel_id=1, source_target_pairs={{0,32},{16,48},{32,0},{48,16},{64,96},{80,112},{96,64},{112,80},{1... | collective-permute-start | bytes 3145736 | tf_op jit(solution)/shard_map/ppermute | solution.py:152
  60.8 7.5 %psum.28 = f32[3,128]{1,0:T(4,128)S(1)} all-reduce(f32[3,128]{1,0:T(4,128)S(1)} %get-tuple-element.23), channel_id=1, replica_groups=mesh['y'=8,'x'=2,'c'=2,'z'=8,'h'=2] {'c'}, use_global_device_ids=true, to_apply=%region_0.1 | all-reduce | flops 384 | bytes 3072 | tf_op jit(solution)/shard_map/psum | solution.py:183
  68.3 17.6 %psum.29 = f32[3,128]{1,0:T(4,128)S(1)} all-reduce(f32[3,128]{1,0:T(4,128)S(1)} %psum.28), channel_id=1, replica_groups=mesh['y'=8,'x'=2,'c'=2,'z'=8,'h'=2] {'z'}, use_global_device_ids=true, to_apply=%region_1.2 | all-reduce | flops 384 | bytes 3072 | tf_op jit(solution)/shard_map/psum | solution.py:184
  85.8 9.5 %psum.30 = f32[3,128]{1,0:T(4,128)S(1)} all-reduce(f32[3,128]{1,0:T(4,128)S(1)} %psum.29), channel_id=1, replica_groups=mesh['y'=8,'x'=2,'c'=2,'z'=8,'h'=2] {'x','h'}, use_global_device_ids=true, to_apply=%region_2.3 | all-reduce | flops 384 | bytes 3072 | tf_op jit(solution)/shard_map/psum | solution.py:185
  95.4 0.0 collective-permute-done.9
  95.4 1.4 %slice_add_fusion = f32[256,1024]{1,0:T(8,128)S(1)} fusion(f32[256,1024]{1,0:T(8,128)} %collective-permute-done.9, f32[512,1024]{1,0:T(8,128)S(1)} %get-tuple-element.22), kind=kLoop, calls=%fused_computation | loop fusion | flops 262144 | bytes 3145728 | tf_op jit(solution)/shard_map/add | solution.py:187
  96.8 6.1 %collective-permute-start.10 = (f32[128,1024]{1,0:T(8,128)S(1)}, f32[128,1024]{1,0:T(8,128)S(1)}, u32[]{:S(2)}, u32[]{:S(2)}) collective-permute-start(f32[128,1024]{1,0:T(8,128)S(1)} %slice.29), channel_id=1, source_target_pairs={{0,16},{16,0},{32,48},{48,32},{64,80},{80,64},{96,112},{112,96},{1... | collective-permute-start | bytes 1572872 | tf_op jit(solution)/shard_map/ppermute | solution.py:152
  102.9 13.1 %psum.31 = f32[3,128]{1,0:T(4,128)S(1)} all-reduce(f32[3,128]{1,0:T(4,128)S(1)} %psum.30), channel_id=1, replica_groups=mesh['y'=8,'x'=2,'c'=2,'z'=8,'h'=2] {'y'}, use_global_device_ids=true, to_apply=%region_4.5 | all-reduce | flops 384 | bytes 3072 | tf_op jit(solution)/shard_map/psum | solution.py:189
  116.0 0.1 reduce_sum.9
  116.1 0.6 fusion.5
  116.7 0.0 collective-permute-done.10
  116.7 0.9 fusion
  117.5 1.6 %reduce-scatter.2.cloned.1.call-done = f32[128,1024]{1,0:T(8,128)} async-done(((f32[1024,1024]{1,0:T(8,128)}), f32[128,1024]{1,0:T(8,128)}) %reduce-scatter.2.cloned.1.call-update) | async-done | bytes 524304 | tf_op jit(solution)/shard_map/reduce_scatter | solution.py:181
  (3 shorter events, 0.1 us)
Async XLA Ops:
  7.2 112.0 %reduce-scatter.2.cloned.1.call-start = ((), (), s32[]{:S(2)}) async-start(), calls=%async_computation.1 | async-start | bytes 4718592 | tf_op jit(solution)/shard_map/reduce_scatter | solution.py:181
  7.2 12.8 %collective-permute-start.2 = (bf16[128,1024]{1,0:T(8,128)(2,1)}, bf16[128,1024]{1,0:T(8,128)(2,1)S(1)}, u32[]{:S(2)}, u32[]{:S(2)}) collective-permute-start(bf16[128,1024]{1,0:T(8,128)(2,1)} %bitcast.31), channel_id=1, source_target_pairs={{0,448},{16,80},{32,480},{48,112},{64,0},{80,144},{96,32},{112,176... | collective-permute-start | bytes 786440 | tf_op jit(solution)/shard_map/ppermute | solution.py:152
  11.3 12.5 %collective-permute-start = (bf16[128,1024]{1,0:T(8,128)(2,1)}, bf16[128,1024]{1,0:T(8,128)(2,1)S(1)}, u32[]{:S(2)}, u32[]{:S(2)}) collective-permute-start(bf16[128,1024]{1,0:T(8,128)(2,1)} %bitcast.37), channel_id=1, source_target_pairs={{0,16},{16,0},{32,48},{48,32},{64,80},{80,64},{96,112},{112,96},{1... | collective-permute-start | bytes 786440 | tf_op jit(solution)/shard_map/ppermute | solution.py:152
  17.9 9.4 %collective-permute-start.6 = (bf16[128,1024]{1,0:T(8,128)(2,1)}, bf16[128,1024]{1,0:T(8,128)(2,1)S(1)}, u32[]{:S(2)}, u32[]{:S(2)}) collective-permute-start(bf16[128,1024]{1,0:T(8,128)(2,1)} %bitcast.32), channel_id=1, source_target_pairs={{0,64},{16,464},{32,96},{48,496},{64,128},{80,16},{96,160},{112,48... | collective-permute-start | bytes 786440 | tf_op jit(solution)/shard_map/ppermute | solution.py:152
  20.0 11.3 %copy-start.1 = (bf16[128,1024]{1,0:T(8,128)(2,1)}, bf16[128,1024]{1,0:T(8,128)(2,1)S(1)}, u32[]{:S(2)}) copy-start(bf16[128,1024]{1,0:T(8,128)(2,1)S(1)} %collective-permute-done.2.rest_3_) | copy-start | bytes 786436
  20.1 11.3 %collective-permute-start.3 = (bf16[128,1024]{1,0:T(8,128)(2,1)S(1)}, bf16[128,1024]{1,0:T(8,128)(2,1)S(1)}, u32[]{:S(2)}, u32[]{:S(2)}) collective-permute-start(bf16[128,1024]{1,0:T(8,128)(2,1)S(1)} %collective-permute-done.2.rest_3_), channel_id=1, source_target_pairs={{0,448},{16,80},{32,480},{48,112},{64,0},{80,144},{96,32},{112,176... | collective-permute-start | bytes 786440 | tf_op jit(solution)/shard_map/ppermute | solution.py:152
  24.7 18.1 %collective-permute-start.1 = (bf16[256,1024]{1,0:T(8,128)(2,1)S(1)}, bf16[256,1024]{1,0:T(8,128)(2,1)S(1)}, u32[]{:S(2)}, u32[]{:S(2)}) collective-permute-start(bf16[256,1024]{1,0:T(8,128)(2,1)S(1)} %pad_maximum_fusion.rest_0_), channel_id=1, source_target_pairs={{0,32},{16,48},{32,0},{48,16},{64,96},{80,112},{96,64},{112,80},{1... | collective-permute-start | bytes 1572872 | tf_op jit(solution)/shard_map/ppermute | solution.py:152
  27.4 8.2 %collective-permute-start.7 = (bf16[128,1024]{1,0:T(8,128)(2,1)S(1)}, bf16[128,1024]{1,0:T(8,128)(2,1)}, u32[]{:S(2)}, u32[]{:S(2)}) collective-permute-start(bf16[128,1024]{1,0:T(8,128)(2,1)S(1)} %collective-permute-done.6.rest_2_), channel_id=1, source_target_pairs={{0,64},{16,464},{32,96},{48,496},{64,128},{80,16},{96,160},{112,48... | collective-permute-start | bytes 786440 | tf_op jit(solution)/shard_map/ppermute | solution.py:152
  30.5 0.7 copy-start.3
  31.4 9.6 %collective-permute-start.4 = (bf16[128,1024]{1,0:T(8,128)(2,1)S(1)}, bf16[128,1024]{1,0:T(8,128)(2,1)S(1)}, u32[]{:S(2)}, u32[]{:S(2)}) collective-permute-start(bf16[128,1024]{1,0:T(8,128)(2,1)S(1)} %collective-permute-done.3.rest_5_), channel_id=1, source_target_pairs={{0,448},{16,80},{32,480},{48,112},{64,0},{80,144},{96,32},{112,176... | collective-permute-start | bytes 786440 | tf_op jit(solution)/shard_map/ppermute | solution.py:152
  33.5 0.7 copy-start.5
  35.6 14.9 %collective-permute-start.8 = (bf16[128,1024]{1,0:T(8,128)(2,1)}, bf16[128,1024]{1,0:T(8,128)(2,1)S(1)}, u32[]{:S(2)}, u32[]{:S(2)}) collective-permute-start(bf16[128,1024]{1,0:T(8,128)(2,1)} %collective-permute-done.7.rest_4_), channel_id=1, source_target_pairs={{0,64},{16,464},{32,96},{48,496},{64,128},{80,16},{96,160},{112,48... | collective-permute-start | bytes 786440 | tf_op jit(solution)/shard_map/ppermute | solution.py:152
  40.9 13.7 %collective-permute-start.5 = (bf16[128,1024]{1,0:T(8,128)(2,1)S(1)}, bf16[128,1024]{1,0:T(8,128)(2,1)S(1)}, u32[]{:S(2)}, u32[]{:S(2)}) collective-permute-start(bf16[128,1024]{1,0:T(8,128)(2,1)S(1)} %collective-permute-done.4.rest_4_), channel_id=1, source_target_pairs={{0,448},{16,80},{32,480},{48,112},{64,0},{80,144},{96,32},{112,176... | collective-permute-start | bytes 786440 | tf_op jit(solution)/shard_map/ppermute | solution.py:152
  42.9 1.0 copy-start.2
  43.8 0.9 copy-start.4
  44.8 0.9 copy-start.6
  45.7 4.8 %copy-start = (bf16[1,128,1024]{2,1,0:T(8,128)(2,1)S(1)}, bf16[1,128,1024]{2,1,0:T(8,128)(2,1)}, u32[]{:S(2)}) copy-start(bf16[1,128,1024]{2,1,0:T(8,128)(2,1)} %param.6) | copy-start | bytes 786436
  57.1 38.2 %collective-permute-start.9 = (f32[256,1024]{1,0:T(8,128)S(1)}, f32[256,1024]{1,0:T(8,128)}, u32[]{:S(2)}, u32[]{:S(2)}) collective-permute-start(f32[256,1024]{1,0:T(8,128)S(1)} %slice.22), channel_id=1, source_target_pairs={{0,32},{16,48},{32,0},{48,16},{64,96},{80,112},{96,64},{112,80},{1... | collective-permute-start | bytes 3145736 | tf_op jit(solution)/shard_map/ppermute | solution.py:152
  96.8 19.9 %collective-permute-start.10 = (f32[128,1024]{1,0:T(8,128)S(1)}, f32[128,1024]{1,0:T(8,128)S(1)}, u32[]{:S(2)}, u32[]{:S(2)}) collective-permute-start(f32[128,1024]{1,0:T(8,128)S(1)} %slice.29), channel_id=1, source_target_pairs={{0,16},{16,0},{32,48},{48,32},{64,80},{80,64},{96,112},{112,96},{1... | collective-permute-start | bytes 1572872 | tf_op jit(solution)/shard_map/ppermute | solution.py:152
Sparse Core Ops, SparseCore 0:
  57.1 61.9 reduce-scatter.1
